TPU v7x, 512 devices: a whole 4x8x8 slice. The times are simulated.
512 devices in a mesh: replica: 32 (over z, y_hi, core), fsdp: 16 (over x, y_lo).
Axes of the slice: x: 4, y: 8 (y_hi: 2, y_lo: 4; y = y_hi * 4 + y_lo), z: 8, core: 2. Of those that a mesh axis runs over, the one named last changes fastest.
Arguments:
- patch_rows: bfloat16 [512, 256, 1792], P(('replica', 'fsdp'))
- qkv_weight: bfloat16 [32, 1792, 2688], P('replica', 'fsdp')
- out_weight: bfloat16 [32, 896, 1792], P('replica', 'fsdp'), may hold values from -0.1875 to 0.1875
- cotangent: bfloat16 [512, 256, 1792], P(('replica', 'fsdp')), may hold values from -6 to 6
- keep_mask: int32 [512, 256], P(('replica', 'fsdp')), may hold values from 0 to 1, as said below
- outer_delta: float32 [32, 2, 524288], P('replica', None, 'fsdp'), may hold values from -6 to 6
- momentum: float32 [2, 524288], P(None, 'fsdp'), may hold values from -6 to 6
- global_params: float32 [2, 524288], P(None, 'fsdp'), may hold values from -6 to 6
- fragment_index: int32 [1], replicated, may hold values from 0 to 1
Outputs:
- layer_out: bfloat16 [512, 256, 1792], P(('replica', 'fsdp'))
- out_grad: float32 [32, 896, 1792], P('replica', 'fsdp')
- new_momentum: float32 [524288], P('fsdp')
- new_params: float32 [524288], P('fsdp')
Inputs may be any that keep to these rules, and one draw needn't show every extreme that they name: `keep_mask`: each image has exactly 154 kept patches.
All inputs are finite; a program needn't handle non-finite values.
Results may differ from a plain program's by a relative error of at most 0.022.
Values may be sent and summed in bfloat16 or wider, within the bound.
A program may use at most 128 MiB of HBM per device.

v0:
```python
import math

import jax
import jax.numpy as jnp
from jax import lax
from jax.sharding import PartitionSpec as P

HSZ = 112
HEADS = 8


EPS = 1e-06


def layer_norm(values):
    floats = values.astype(jnp.float32)
    centre = jnp.mean(floats, axis=-1, keepdims=True)
    shifted = floats - centre
    spread = jnp.mean(shifted * shifted, axis=-1, keepdims=True)
    return (shifted * lax.rsqrt(spread + EPS)).astype(jnp.bfloat16)


def attend(qkv_rows, valid):
    query = qkv_rows[:, :, 0]
    keys = qkv_rows[:, :, 1]
    value_rows = qkv_rows[:, :, 2]
    scores = jnp.einsum("iqhd,ikhd->ihqk", query, keys, preferred_element_type=jnp.float32) * (
        1.0 / math.sqrt(HSZ)
    )
    scores = jnp.where(valid[:, None, None, :] > 0, scores, -1e30)
    peak = jnp.max(scores, axis=-1, keepdims=True)
    expo = jnp.exp(scores - peak)
    total = jnp.sum(expo, axis=-1, keepdims=True)
    probs = (expo / total).astype(jnp.bfloat16)
    mixed = jnp.einsum(
        "ihqk,ikhd->iqhd", probs, value_rows, preferred_element_type=jnp.float32
    ).astype(jnp.bfloat16)
    mixed = mixed.reshape(mixed.shape[0], mixed.shape[1], HEADS * HSZ)
    mixed = mixed * valid[:, :, None].astype(jnp.bfloat16)
    return mixed


def on_device(
    patch_rows,
    qkv_weight,
    out_weight,
    cotangent,
    keep_mask,
    outer_delta,
    momentum,
    global_params,
    fragment_index,
):
    index = fragment_index[0]
    local_delta = lax.dynamic_index_in_dim(outer_delta[0], index, 0, keepdims=False)
    old_momentum = lax.dynamic_index_in_dim(momentum, index, 0, keepdims=False)
    old_params = lax.dynamic_index_in_dim(global_params, index, 0, keepdims=False)
    summed = lax.psum(local_delta.astype(jnp.bfloat16), "replica").astype(jnp.float32)
    average = summed / lax.axis_size("replica")
    new_momentum = 0.9 * old_momentum + average
    new_params = old_params - 0.7 * (average + 0.9 * new_momentum)
    images, patches, width = patch_rows.shape
    row_count = patch_rows.shape[1]
    normed = layer_norm(patch_rows.reshape(images * row_count, width))
    whole_qkv = lax.all_gather(qkv_weight[0], "fsdp", axis=0, tiled=True)
    projected = jnp.dot(normed, whole_qkv, preferred_element_type=jnp.float32).astype(jnp.bfloat16)
    attended = attend(projected.reshape(images, row_count, 3, HEADS, HSZ), keep_mask)
    flat_attended = attended.reshape(images * row_count, HEADS * HSZ)
    whole_out = lax.all_gather(out_weight[0], "fsdp", axis=0, tiled=True)
    result = jnp.dot(flat_attended, whole_out, preferred_element_type=jnp.float32).astype(
        jnp.bfloat16
    )
    result = result.reshape(images, row_count, width)
    flat_grads = cotangent.reshape(images * row_count, width)
    out_grad = lax.psum_scatter(
        lax.dot_general(
            flat_attended, flat_grads, (((0,), (0,)), ((), ())), preferred_element_type=jnp.float32
        ).astype(jnp.bfloat16),
        "fsdp",
        scatter_dimension=0,
        tiled=True,
    ).astype(jnp.float32)
    return (result, out_grad[None], new_momentum, new_params)


def solution(mesh):
    in_specs = (
        P(("replica", "fsdp"), None, None),
        P("replica", "fsdp", None),
        P("replica", "fsdp", None),
        P(("replica", "fsdp"), None, None),
        P(("replica", "fsdp"), None),
        P("replica", None, "fsdp"),
        P(None, "fsdp"),
        P(None, "fsdp"),
        P(),
    )
    out_specs = (
        P(("replica", "fsdp"), None, None),
        P("replica", "fsdp", None),
        P("fsdp"),
        P("fsdp"),
    )
    return jax.shard_map(
        on_device, mesh=mesh, in_specs=in_specs, out_specs=out_specs, check_vma=False
    )
```

profile of v0, /device:TPU:56, one launch (start us, length us, event | category | flops | bytes accessed | tf_op | source)
XLA Modules:
  0.0 481.2 jit_solution(15852729770017195764)
XLA Ops:
  8.1 0.7 all-gather.5.cloned.1.call-update
  8.8 0.0 all-reduce.2.cloned.1.call-start
  9.5 2.0 convert_reduce_fusion.1
  11.4 0.0 all-gather.7.cloned.1.call-start
  11.5 0.7 all-gather.7.cloned.1.call-update
  12.2 0.0 reduce-scatter.2.cloned.1.call-start
  12.2 0.7 convert_reduce_fusion.2
  12.9 0.7 compare_reduce_fusion
  13.6 1.4 convert_reduce_fusion
  15.0 0.4 fusion.18
  15.4 217.4 %all-gather.5.cloned.1.call-done = bf16[1,1792,2688]{2,1,0:T(8,128)(2,1)} async-done(((bf16[1,112,2688]{2,1,0:T(8,128)(2,1)}), bf16[1,1792,2688]{2,1,0:T(8,128)(2,1)}) %all-gather.5.cloned.1.call-update) | async-done | bytes 9633808 | tf_op jit(solution)/shard_map/all_gather | solution.py:65
  232.9 7.7 %fusion.3 = bf16[256,2688]{1,0:T(8,128)(2,1)} fusion(bf16[1,1792,2688]{2,1,0:T(8,128)(2,1)} %all-gather.5.cloned.1.call-done, bf16[1,256,1792]{2,1,0:T(8,128)(2,1)S(1)} %copy-done.1, f32[256]{0:T(256)S(1)} %add_rsqrt_fusion, f32[256]{0:T(256)S(1)} %broadcast_multiply_fusion), kind=kOutput, calls=%fused_computation.3 | convolution fusion | flops 2468773888 | bytes 11929600 | tf_op jit(solution)/shard_map/dot_general | solution.py:66
  240.6 1.8 copy.17
  242.4 0.9 fusion.37
  243.3 1.1 bitcast_multiply_fusion.1
  244.5 2.7 convolution_convert_fusion
  247.2 0.9 copy-done.2
  248.1 0.1 copy-done.3
  248.2 0.3 dynamic-slice_multiply_fusion
  248.5 218.3 %all-reduce.2.cloned.1.call-done = bf16[32768]{0:T(1024)(128)(2,1)} async-done(((bf16[32768]{0:T(1024)(128)(2,1)}), bf16[32768]{0:T(1024)(128)(2,1)}) %all-reduce.2.cloned.1.call-update) | async-done | bytes 65552 | tf_op jit(solution)/shard_map/psum | solution.py:58
  466.8 1.6 multiply_subtract_fusion
  468.3 0.1 bitcast_multiply_fusion
  468.4 4.0 fusion.11
  472.4 1.7 bitcast_convert_fusion
  (13 shorter events, 0.1 us)
Async XLA Ops:
  8.0 236.5 %copy-start = (bf16[1,256,1792]{2,1,0:T(8,128)(2,1)S(1)}, bf16[1,256,1792]{2,1,0:T(8,128)(2,1)}, u32[]{:S(2)}) copy-start(bf16[1,256,1792]{2,1,0:T(8,128)(2,1)} %param.12) | copy-start | bytes 2752516
  8.0 7.0 %copy-start.1 = (bf16[1,256,1792]{2,1,0:T(8,128)(2,1)S(1)}, bf16[1,256,1792]{2,1,0:T(8,128)(2,1)}, u32[]{:S(2)}) copy-start(bf16[1,256,1792]{2,1,0:T(8,128)(2,1)} %param.9) | copy-start | bytes 2752516
  8.0 224.9 %all-gather.5.cloned.1.call-start = ((), (), s32[]{:S(2)}) async-start(), calls=%async_computation.3 | async-start | bytes 10235904 | tf_op jit(solution)/shard_map/all_gather | solution.py:65
  8.8 458.0 %all-reduce.2.cloned.1.call-start = ((), (), s32[]{:S(2)}) async-start(), calls=%async_computation.2 | async-start | bytes 131072 | tf_op jit(solution)/shard_map/psum | solution.py:58
  11.4 457.0 %all-gather.7.cloned.1.call-start = ((), (), s32[]{:S(2)}) async-start(), calls=%async_computation.4 | async-start | bytes 3411968 | tf_op jit(solution)/shard_map/all_gather | solution.py:69
  12.2 460.2 %reduce-scatter.2.cloned.1.call-start = ((), (), s32[]{:S(2)}) async-start(), calls=%async_computation.1 | async-start | bytes 3411968 | tf_op jit(solution)/shard_map/reduce_scatter | solution.py:75
  247.1 0.9 copy-start.2
  247.1 1.0 copy-start.3
Sparse Core Ops, SparseCore 0:
  10.9 221.8 all-gather.4
  235.0 88.4 all-gather.6
  326.3 94.7 reduce-scatter.1
Sparse Core Ops, SparseCore 1:
  12.7 454.0 all-reduce.1
where the time goes:
time: 486 us; the launch traced here: 481 us
  waiting for transfers between devices  437 us (90%)
  matrix products  16.4 us (3%)
  between operations  15.9 us (3%)
  other arithmetic  6.81 us (1%)
    psum x1, waiting for transfers between devices, on_device(): lax.psum(local_delta.astype(jnp.bfloat16), 'replica').astype(jnp.float32)  218 us
    all_gather x1, waiting for transfers between devices, on_device(): whole_qkv = lax.all_gather(qkv_weight[0], 'fsdp', axis=0, tiled=True)  217 us
  transfers between devices with their start and end apart: 4, of which 2 were waited for; matrix products, arithmetic and copies ran while one was open for 5% of the time, Pallas kernels for 0%

commit v1 on v0

v1 whole, which is shorter than its diff:
```python
import math

import jax
import jax.numpy as jnp
from jax import lax
from jax.experimental import pallas as pl
from jax.experimental.pallas import tpu as pltpu
from jax.sharding import PartitionSpec as P

HSZ = 112
HEADS = 8
KEEP = 154
ROWS = 160
HALF = ROWS // 2
NX = 4
NY = 4
EPS = 1e-06
MESH = pl.DeviceIdType.MESH
F32 = jnp.float32
BF16 = jnp.bfloat16


def dot(a, b, dims=(((1,), (0,)), ((), ()))):
    return lax.dot_general(a, b, dims, preferred_element_type=F32)


def kernel(
    patch_ref, qkvw_ref, outw_ref, cot_ref, mask_ref, delta_ref, mom_ref, par_ref,
    out_ref, grad_ref, newm_ref, newp_ref,
    pick, wpack, wbuf, act, cotb, owbuf, qkv, att, lo_send, lo_recv, g_send, g_recv,
    sum1, sum2, rec1, rec2, rec3, total,
    wx_s, wx_r, wy_s, wy_r, wf_s, ax_s, ax_r, cx_s, cx_r, oy_s, oy_r, of_s,
    lx_s, lx_r, gy_s, gy_r, pc_s, pc_r, z1_s, z1_r, z2_s, z2_r,
):
    r = lax.axis_index("replica")
    f = lax.axis_index("fsdp")
    nz = lax.axis_size("replica") // 4
    core, y_hi, z = lax.rem(r, 2), lax.rem(r // 2, 2), r // 4
    x, y = f // NY, lax.rem(f, NY)
    r_core = r + 1 - 2 * core
    r_yhi = r + 2 - 4 * y_hi

    def at_x(k):
        return lax.rem(x + k, NX)

    def at_y(k):
        return lax.rem(y + k, NY)

    def dev_x(k):
        return (r, at_x(k) * NY + y)

    def dev_y(yy):
        return (r, x * NY + yy)

    def dev_z(k):
        return (lax.rem(z + k, nz) * 4 + lax.rem(r, 4), f)

    def remote(src, dst, s, t, dev):
        return pltpu.make_async_remote_copy(
            src_ref=src, dst_ref=dst, send_sem=s, recv_sem=t, device_id=dev, device_id_type=MESH
        )

    barrier = pltpu.get_barrier_semaphore()
    partners = [dev_x(k) for k in (1, 2, 3)] + [dev_y(at_y(k)) for k in (1, 2, 3)]
    partners += [(r_core, f), (r_yhi, f)] + [dev_z(k) for k in range(1, nz)]
    for dev in partners:
        pl.semaphore_signal(barrier, inc=1, device_id=dev, device_id_type=MESH)

    for k in range(NX):
        start = min(224 * k // 128, 4) * 128
        row = lax.broadcasted_iota(jnp.int32, (384, 256), 0)
        lane = lax.broadcasted_iota(jnp.int32, (384, 256), 1)
        wanted = 224 * k - start + 56 * (lane // 64) + lane % 64
        chosen = jnp.where((row == wanted) & (lane % 64 < 56), 1.0, 0.0).astype(BF16)
        for t in range(3):
            cols = qkvw_ref[:, 896 * t + start : 896 * t + start + 384]
            wpack[k, :, 256 * t : 256 * t + 256] = dot(cols, chosen).astype(BF16)
    wbuf[f] = wpack[x]
    owbuf[y, 0:56, :] = outw_ref[...]
    owbuf[y, 56:64, :] = jnp.zeros((8, outw_ref.shape[1]), BF16)

    pl.semaphore_wait(barrier, len(partners))

    def w_x(k):
        return remote(wpack.at[at_x(k)], wbuf.at[f], wx_s.at[k], wx_r.at[NX - k], dev_x(k))

    def w_x_in(k):
        slot = wbuf.at[at_x(k) * NY + y]
        return remote(slot, slot, wx_s.at[NX - k], wx_r.at[k], dev_x(k))

    def along_y(buf, send, recv, fwd):
        def out(k):
            to = at_y(k)
            return remote(buf(y), buf(y), send(k), recv(y), dev_y(to))

        def near(k):
            return jnp.abs(at_y(k) - y) < 3

        def start():
            for k in (1, 3, 2):
                pl.when(near(k))(lambda k=k: out(k).start())

        def forward():
            def from_low():
                remote(buf(0), buf(0), fwd, recv(0), dev_y(3)).wait_recv()
                remote(buf(0), buf(0), fwd, recv(0), dev_y(3)).start()

            def from_high():
                remote(buf(3), buf(3), fwd, recv(3), dev_y(0)).wait_recv()
                remote(buf(3), buf(3), fwd, recv(3), dev_y(0)).start()

            pl.when(y == 2)(from_low)
            pl.when(y == 1)(from_high)

        def finish():
            for k in (1, 2, 3):
                src = at_y(k)
                done = ((y == 2) & (src == 0)) | ((y == 1) & (src == 3))
                pl.when(jnp.logical_not(done))(
                    lambda src=src: remote(buf(src), buf(src), fwd, recv(src), dev_y(src)).wait_recv()
                )

        def drain():
            for k in (1, 3, 2):
                pl.when(near(k))(lambda k=k: out(k).wait_send())
            pl.when((y == 1) | (y == 2))(
                lambda: remote(buf(y), buf(y), fwd, recv(y), dev_y(at_y(1))).wait_send()
            )

        return start, forward, finish, drain

    w_y = [
        along_y(
            lambda yy, k=k: wbuf.at[at_x(k) * NY + yy],
            lambda j, k=k: wy_s.at[k, j],
            lambda yy, k=k: wy_r.at[k, yy],
            wf_s.at[k],
        )
        for k in range(NX)
    ]
    o_y = along_y(lambda yy: owbuf.at[yy], lambda j: oy_s.at[j], lambda yy: oy_r.at[yy], of_s)

    for k in (2, 1, 3):
        w_x(k).start()
    w_y[0][0]()

    mask = mask_ref[...]
    n = mask.shape[1]
    upper = (
        lax.broadcasted_iota(jnp.int32, (n, n), 0) <= lax.broadcasted_iota(jnp.int32, (n, n), 1)
    )
    place = dot(
        jnp.broadcast_to(mask, (16, n)).astype(F32).astype(BF16),
        jnp.where(upper, 1.0, 0.0).astype(BF16),
    )[0:1, :].astype(jnp.int32)
    place = jnp.where(mask > 0, place - 1, -1)
    pick[...] = jnp.where(
        lax.broadcasted_iota(jnp.int32, (ROWS, n), 0) == place, 1.0, 0.0
    ).astype(BF16)
    kept = dot(pick[...], patch_ref[...])
    shifted = kept - jnp.mean(kept, axis=-1, keepdims=True)
    spread = jnp.mean(shifted * shifted, axis=-1, keepdims=True)
    act[x] = (shifted * lax.rsqrt(spread + EPS)).astype(BF16)

    low, high = pl.ds(0, HALF), pl.ds(HALF, HALF)

    def along_x(buf, send, recv):
        def move(i, who, rows, to):
            return remote(buf.at[who, rows], buf.at[who, rows], send.at[i], recv.at[i], dev_x(to))

        def own():
            return [move(0, x, low, 1), move(1, x, high, 3), move(2, x, high, 1), move(3, x, low, 3)]

        def passing():
            return [move(4, at_x(3), low, 1), move(5, at_x(1), high, 3)]

        def incoming():
            return [
                move(0, at_x(3), low, 3), move(1, at_x(1), high, 1),
                move(2, at_x(3), high, 3), move(3, at_x(1), low, 1),
                move(4, at_x(2), low, 2), move(5, at_x(2), high, 2),
            ]

        def start():
            for c in own():
                c.start()

        def forward():
            got = incoming()
            for i in (0, 1):
                got[i].wait_recv()
                passing()[i].start()

        def finish():
            for c in incoming()[2:]:
                c.wait_recv()

        def drain():
            for c in own() + passing():
                c.wait_send()

        return start, forward, finish, drain

    a_x = along_x(act, ax_s, ax_r)
    c_x = along_x(cotb, cx_s, cx_r)
    a_x[0]()

    def rows8(at, size):
        return pl.ds(pl.multiple_of(at, 8), size)

    pair1 = remote(delta_ref.at[rows8(128 * (1 - core), 128)], rec1, pc_s.at[0], pc_r.at[0], (r_core, f))
    pair1.start()

    for k in (1, 3, 2):
        w_x_in(k).wait_recv()
        w_y[k][0]()

    cotb[x] = dot(pick[...], cot_ref[...]).astype(BF16)
    pair1.wait_recv()
    sum1[...] = delta_ref[rows8(128 * core, 128), :] + rec1[...]
    pair2 = remote(sum1.at[rows8(64 * (1 - y_hi), 64)], rec2, pc_s.at[1], pc_r.at[1], (r_yhi, f))
    pair2.start()

    a_x[1]()
    w_y[0][1]()
    c_x[0]()
    pair2.wait_recv()
    sum2[...] = sum1[rows8(64 * y_hi, 64), :] + rec2[...]

    def z_out(k):
        to = lax.rem(z + k, nz)
        return remote(sum2.at[rows8(8 * to, 8)], rec3.at[nz - k], z1_s.at[k], z1_r.at[nz - k], dev_z(k))

    for k in range(1, nz):
        z_out(k).start()
    w_y[1][1]()
    w_y[3][1]()

    def z_in(k):
        return remote(rec3.at[k], rec3.at[k], z1_s.at[nz - k], z1_r.at[k], dev_z(k))

    mine = sum2[rows8(8 * z, 8), :]
    for k in range(1, nz):
        z_in(k).wait_recv()
        mine = mine + rec3[k]
    base = 128 * core + 64 * y_hi
    total[rows8(base + 8 * z, 8), :] = mine

    def z_back(k):
        part = total.at[rows8(base + 8 * z, 8)]
        return remote(part, part, z2_s.at[k], z2_r.at[nz - k], dev_z(k))

    def z_back_in(k):
        part = total.at[rows8(base + 8 * lax.rem(z + k, nz), 8)]
        return remote(part, part, z2_s.at[nz - k], z2_r.at[k], dev_z(k))

    for k in range(1, nz):
        z_back(k).start()
    w_y[2][1]()
    o_y[0]()
    c_x[1]()

    for k in range(1, nz):
        z_back_in(k).wait_recv()

    def two_out(i, at, size, dev):
        part = total.at[rows8(at, size)]
        return remote(part, part, pc_s.at[i], pc_r.at[i], dev)

    pair3 = two_out(2, base, 64, (r_yhi, f))
    pair3.start()
    two_out(2, 128 * core + 64 * (1 - y_hi), 64, (r_yhi, f)).wait_recv()
    pair4 = two_out(3, 128 * core, 128, (r_core, f))
    pair4.start()
    two_out(3, 128 * (1 - core), 128, (r_core, f)).wait_recv()
    average = total[...] * (1.0 / 32.0)
    new_m = 0.9 * mom_ref[...] + average
    newm_ref[...] = new_m
    newp_ref[...] = par_ref[...] - 0.7 * (average + 0.9 * new_m)
    o_y[1]()

    a_x[2]()
    for k in range(NX):
        w_y[k][2]()
    width = act.shape[2]
    qkv[...] = dot(
        act[...].reshape(NX * ROWS, width), wbuf[...].reshape(width, 768)
    ).astype(BF16).reshape(NX, ROWS, 768)

    def attend(i, carry):
        for h in range(2):
            q = qkv[i, :, 128 * h : 128 * h + 128]
            key = qkv[i, :, 256 + 128 * h : 384 + 128 * h]
            val = qkv[i, :, 512 + 128 * h : 640 + 128 * h]
            scores = dot(q, key, (((1,), (1,)), ((), ()))) * (1.0 / math.sqrt(HSZ))
            col = lax.broadcasted_iota(jnp.int32, (ROWS, ROWS), 1)
            scores = jnp.where(col < KEEP, scores, -1e30)
            expo = jnp.exp(scores - jnp.max(scores, axis=-1, keepdims=True))
            probs = (expo / jnp.sum(expo, axis=-1, keepdims=True)).astype(BF16)
            att[i, :, 128 * h : 128 * h + 128] = dot(probs, val).astype(BF16)
        return carry

    lax.fori_loop(0, NX, attend, 0)

    o_y[2]()
    def project(i, carry):
        lo_send[i] = dot(att[i], owbuf[...].reshape(NY * 64, width)).astype(BF16)
        return carry

    lax.fori_loop(0, NX, project, 0)

    def lo_out(k):
        return remote(lo_send.at[at_x(k)], lo_recv.at[NX - k], lx_s.at[k], lx_r.at[NX - k], dev_x(k))

    def lo_in(k):
        return remote(lo_recv.at[k], lo_recv.at[k], lx_s.at[NX - k], lx_r.at[k], dev_x(k))

    for k in (2, 1, 3):
        lo_out(k).start()

    c_x[2]()
    g_send[...] = dot(
        att[...].reshape(NX * ROWS, 256), cotb[...].reshape(NX * ROWS, width), (((0,), (0,)), ((), ()))
    ).astype(BF16).reshape(NY, 64, width)

    def g_out(k):
        return remote(g_send.at[at_y(k)], g_recv.at[NY - k], gy_s.at[k], gy_r.at[NY - k], dev_y(at_y(k)))

    def g_in(k):
        return remote(g_recv.at[k], g_recv.at[k], gy_s.at[NY - k], gy_r.at[k], dev_y(at_y(k)))

    for k in (2, 1, 3):
        g_out(k).start()

    whole = g_send[y].astype(F32)
    for k in (1, 2, 3):
        g_in(k).wait_recv()
        whole = whole + g_recv[k].astype(F32)
    grad_ref[...] = whole[0:56, :]

    result = lo_send[x].astype(F32)
    for k in (1, 3, 2):
        lo_in(k).wait_recv()
        result = result + lo_recv[k].astype(F32)
    out_ref[...] = dot(pick[...], result.astype(BF16), (((0,), (0,)), ((), ()))).astype(BF16)

    for k in (1, 2, 3):
        w_x(k).wait_send()
        lo_out(k).wait_send()
        g_out(k).wait_send()
    for k in range(NX):
        w_y[k][3]()
    o_y[3]()
    a_x[3]()
    c_x[3]()
    for c in (pair1, pair2, pair3, pair4):
        c.wait_send()
    for k in range(1, nz):
        z_out(k).wait_send()
        z_back(k).wait_send()


def on_device(
    patch_rows, qkv_weight, out_weight, cotangent, keep_mask, outer_delta, momentum, global_params,
    fragment_index,
):
    index = fragment_index[0]
    delta = lax.dynamic_index_in_dim(outer_delta[0], index, 0, keepdims=False).reshape(256, 128)
    old_m = lax.dynamic_index_in_dim(momentum, index, 0, keepdims=False).reshape(256, 128)
    old_p = lax.dynamic_index_in_dim(global_params, index, 0, keepdims=False).reshape(256, 128)
    width = patch_rows.shape[2]
    nz = lax.axis_size("replica") // 4
    vmem = pl.BlockSpec(memory_space=pltpu.VMEM)
    sem = pltpu.SemaphoreType.DMA
    shapes = [
        jax.ShapeDtypeStruct((256, width), BF16),
        jax.ShapeDtypeStruct((56, width), F32),
        jax.ShapeDtypeStruct((256, 128), F32),
        jax.ShapeDtypeStruct((256, 128), F32),
    ]
    out, grad, new_m, new_p = pl.pallas_call(
        kernel,
        out_shape=shapes,
        in_specs=[vmem] * 8,
        out_specs=[vmem] * 4,
        scratch_shapes=[
            pltpu.VMEM((ROWS, 256), BF16),
            pltpu.VMEM((NX, 112, 768), BF16),
            pltpu.VMEM((NX * NY, 112, 768), BF16),
            pltpu.VMEM((NX, ROWS, width), BF16),
            pltpu.VMEM((NX, ROWS, width), BF16),
            pltpu.VMEM((NY, 64, width), BF16),
            pltpu.VMEM((NX, ROWS, 768), BF16),
            pltpu.VMEM((NX, ROWS, 256), BF16),
            pltpu.VMEM((NX, ROWS, width), BF16),
            pltpu.VMEM((NX, ROWS, width), BF16),
            pltpu.VMEM((NY, 64, width), BF16),
            pltpu.VMEM((NY, 64, width), BF16),
            pltpu.VMEM((128, 128), F32),
            pltpu.VMEM((64, 128), F32),
            pltpu.VMEM((128, 128), F32),
            pltpu.VMEM((64, 128), F32),
            pltpu.VMEM((nz, 8, 128), F32),
            pltpu.VMEM((256, 128), F32),
            sem((NX,)), sem((NX,)),
            sem((NX, NY)), sem((NX, NY)), sem((NX,)),
            sem((6,)), sem((6,)), sem((6,)), sem((6,)),
            sem((NY,)), sem((NY,)), sem,
            sem((NX,)), sem((NX,)), sem((NY,)), sem((NY,)),
            sem((4,)), sem((4,)), sem((nz,)), sem((nz,)), sem((nz,)), sem((nz,)),
        ],
        compiler_params=pltpu.CompilerParams(
            collective_id=0, has_side_effects=True, vmem_limit_bytes=48 * 1024 * 1024
        ),
    )(
        patch_rows[0], qkv_weight[0], out_weight[0], cotangent[0], keep_mask, delta, old_m, old_p
    )
    return out[None], grad[None], new_m.reshape(-1), new_p.reshape(-1)


def solution(mesh):
    in_specs = (
        P(("replica", "fsdp"), None, None),
        P("replica", "fsdp", None),
        P("replica", "fsdp", None),
        P(("replica", "fsdp"), None, None),
        P(("replica", "fsdp"), None),
        P("replica", None, "fsdp"),
        P(None, "fsdp"),
        P(None, "fsdp"),
        P(),
    )
    out_specs = (
        P(("replica", "fsdp"), None, None),
        P("replica", "fsdp", None),
        P("fsdp"),
        P("fsdp"),
    )
    return jax.shard_map(
        on_device, mesh=mesh, in_specs=in_specs, out_specs=out_specs, check_vma=False
    )
```

time: 486 us -> 125 us (0.26)
  waiting for transfers between devices: 437 us -> 0 us
  Pallas kernels: 0 us -> 116 us
  matrix products: 16.4 us -> 0 us
  between operations: 15.9 us -> 1.42 us
  other arithmetic: 6.81 us -> 0 us
    psum x1 -> x0, waiting for transfers between devices: 218 us -> none  [on_device(): lax.psum(local_delta.astype(jnp.bfloat16), 'replica').astype(jnp.float32)]
    all_gather x2 -> x0, waiting for transfers between devices: 217 us -> none  [the longest x1 217 us: on_device(): whole_qkv = lax.all_gather(qkv_weight[0], 'fsdp', axis=0, tiled=True)]
    pallas_call x0 -> x1, Pallas kernels: none -> 116 us  [on_device(): pl.pallas_call(kernel, out_shape=shapes, in_specs=[vmem] * 8, out_specs=[...]
    dot_general x4 -> x0, matrix products: 15.5 us -> none  [the longest x1 7.75 us: on_device(): jnp.dot(normed, whole_qkv, preferred_element_type=jnp.float32)]
    unnamed x8 -> x16, local copies, waits for them, and re-layouts: 1.02 us -> 6.23 us
  transfers between devices with their start and end apart: 4 -> 0, of which waited for: 2 -> 0; matrix products, arithmetic and copies ran while one was open for 5% -> 0% of each run, Pallas kernels for 0% -> 0%
where the time goes in v1:
time: 125 us
  Pallas kernels  116 us (93%)
  local copies, waits for them, and re-layouts  7.69 us (6%)
  between operations  1.42 us (1%)
    pallas_call x1, Pallas kernels, on_device(): pl.pallas_call(kernel, out_shape=shapes, in_specs=[vmem] * 8, out_specs=[...  116 us
    unnamed x16, local copies, waits for them, and re-layouts  6.23 us

profile of v1, /device:TPU:56, one launch (start us, length us, event | category | flops | bytes accessed | tf_op | source)
XLA Modules:
  0.0 124.9 jit_solution(2964837556033863577)
XLA Ops:
  0.6 0.0 copy-start
  0.6 0.0 copy-start.3
  1.4 0.2 copy-done
  1.6 0.1 constant_dynamic-slice_fusion.2
  1.7 0.0 copy-start.4
  1.7 1.3 %constant_dynamic-slice_fusion = (f32[1,32768]{1,0:T(1,128)S(1)}, f32[1,32768]{1,0:T(1,128)S(1)}) fusion(f32[2,32768]{1,0:T(2,128)} %param.16, s32[]{:T(128)S(6)} %select_n.6, f32[2,32768]{1,0:T(2,128)} %param.15), kind=kLoop, calls=%fused_computation | loop fusion | bytes 524292 | tf_op jit(solution)/shard_map/jit(dynamic_index_in_dim)/dynamic_slice | solution.py:370
  3.1 0.0 copy-start.5
  3.1 0.0 copy-done.3
  3.1 0.0 copy-done.4
  3.1 0.7 copy-done.5
  3.7 0.0 copy-start.1
  3.7 1.2 copy-done.1
  4.9 0.0 copy-start.2
  4.9 1.2 copy-done.2
  6.1 115.7 %shard_map.120 = (bf16[256,1792]{1,0:T(8,128)(2,1)S(1)}, f32[56,1792]{1,0:T(8,128)S(1)}, f32[256,128]{1,0:T(8,128)S(1)}, f32[256,128]{1,0:T(8,128)S(1)}) custom-call(bf16[256,1792]{1,0:T(8,128)(2,1)S(1)} %bitcast.16, bf16[112,2688]{1,0:T(8,128)(2,1)S(1)} %bitcast.18, bf16[56,1792]{1,0:T(8,128)(2,1)S(1)} %bitcast.23, bf16[256,1792]{1,0:T(8,128)(2,1)S(1)} %bitcast.17, ...), custom_call_target="tpu_custom_call" | custom-call | tf_op jit(solution)/shard_map/pallas_call | solution.py:381
  121.9 0.9 copy.18
  122.8 0.7 copy.19
  123.5 0.7 copy.20
  124.2 0.7 copy.21
Async XLA Ops:
  0.6 1.0 copy-start
  0.6 2.4 %copy-start.3 = (bf16[1,112,2688]{2,1,0:T(8,128)(2,1)S(1)}, bf16[1,112,2688]{2,1,0:T(8,128)(2,1)}, u32[]{:S(2)}) copy-start(bf16[1,112,2688]{2,1,0:T(8,128)(2,1)} %param.10) | copy-start | bytes 1806340
  1.7 1.4 %copy-start.4 = (bf16[1,56,1792]{2,1,0:T(8,128)(2,1)S(1)}, bf16[1,56,1792]{2,1,0:T(8,128)(2,1)}, u32[]{:S(2)}) copy-start(bf16[1,56,1792]{2,1,0:T(8,128)(2,1)} %param.11) | copy-start | bytes 602116
  3.1 0.7 copy-start.5
  3.7 1.2 copy-start.1
  4.9 1.2 copy-start.2

commit v2 on v1

--- a/solution.py
+++ b/solution.py
@@ -25,20 +25,32 @@
 
 
 def kernel(
-    patch_ref, qkvw_ref, outw_ref, cot_ref, mask_ref, delta_ref, mom_ref, par_ref,
+    patch_hbm, qkvw_hbm, outw_hbm, cot_hbm, delta_hbm, mom_hbm, par_hbm, mask_ref, index_ref,
     out_ref, grad_ref, newm_ref, newp_ref,
-    pick, wpack, wbuf, act, cotb, owbuf, qkv, att, lo_send, lo_recv, g_send, g_recv,
-    sum1, sum2, rec1, rec2, rec3, total,
+    patch_ref, qkvw_ref, outw_ref, cot_ref, delta_ref, mom_ref, par_ref,
+    local, piece, from_y, parts, total,
+    pick, wpack, wbuf, act, cotb, owbuf, qkv, att, lo_send, lo_recv, lo_mid, g_send, g_recv, g_mid,
     wx_s, wx_r, wy_s, wy_r, wf_s, ax_s, ax_r, cx_s, cx_r, oy_s, oy_r, of_s,
-    lx_s, lx_r, gy_s, gy_r, pc_s, pc_r, z1_s, z1_r, z2_s, z2_r,
+    lx_s, lx_r, gy_s, gy_r, gm_s, gm_r, in_s, z1_s, z1_r, z2_s, z2_r, yh_s, yh_r,
 ):
     r = lax.axis_index("replica")
     f = lax.axis_index("fsdp")
-    nz = lax.axis_size("replica") // 4
-    core, y_hi, z = lax.rem(r, 2), lax.rem(r // 2, 2), r // 4
     x, y = f // NY, lax.rem(f, NY)
-    r_core = r + 1 - 2 * core
-    r_yhi = r + 2 - 4 * y_hi
+    pieces = lax.axis_size("replica") // 2
+    own = r // 4 * 2 + lax.rem(r, 2)
+    y_hi = lax.rem(r // 2, 2)
+
+    loads = [
+        pltpu.make_async_copy(src, dst, in_s.at[i])
+        for i, (src, dst) in enumerate(
+            [
+                (qkvw_hbm, qkvw_ref), (patch_hbm, patch_ref), (outw_hbm, outw_ref), (cot_hbm, cot_ref),
+                (delta_hbm, delta_ref), (mom_hbm, mom_ref), (par_hbm, par_ref),
+            ]
+        )
+    ]
+    for i in (0, 4, 1, 3, 2, 5, 6):
+        loads[i].start()
 
     def at_x(k):
         return lax.rem(x + k, NX)
@@ -52,8 +64,9 @@
     def dev_y(yy):
         return (r, x * NY + yy)
 
-    def dev_z(k):
-        return (lax.rem(z + k, nz) * 4 + lax.rem(r, 4), f)
+    def dev_p(k):
+        to = lax.rem(own + k, pieces)
+        return (to // 2 * 4 + y_hi * 2 + lax.rem(to, 2), f)
 
     def remote(src, dst, s, t, dev):
         return pltpu.make_async_remote_copy(
@@ -62,10 +75,11 @@
 
     barrier = pltpu.get_barrier_semaphore()
     partners = [dev_x(k) for k in (1, 2, 3)] + [dev_y(at_y(k)) for k in (1, 2, 3)]
-    partners += [(r_core, f), (r_yhi, f)] + [dev_z(k) for k in range(1, nz)]
+    partners += [(r + 2 - 4 * y_hi, f)] + [dev_p(k) for k in range(1, pieces)]
     for dev in partners:
         pl.semaphore_signal(barrier, inc=1, device_id=dev, device_id_type=MESH)
 
+    loads[0].wait()
     for k in range(NX):
         start = min(224 * k // 128, 4) * 128
         row = lax.broadcasted_iota(jnp.int32, (384, 256), 0)
@@ -76,9 +90,32 @@
             cols = qkvw_ref[:, 896 * t + start : 896 * t + start + 384]
             wpack[k, :, 256 * t : 256 * t + 256] = dot(cols, chosen).astype(BF16)
     wbuf[f] = wpack[x]
-    owbuf[y, 0:56, :] = outw_ref[...]
-    owbuf[y, 56:64, :] = jnp.zeros((8, outw_ref.shape[1]), BF16)
-
+
+    def synced(ref):
+        return jnp.where(jnp.full((256, 128), index_ref[0], jnp.int32) == 0, ref[:, 0, :], ref[:, 1, :])
+
+    loads[4].wait()
+    local[...] = synced(delta_ref)
+
+    def rows_of(k):
+        return pl.ds(pl.multiple_of(16 * lax.rem(own + k, pieces), 16), 16)
+
+    def part_out(k):
+        at = pieces - k
+        return remote(local.at[rows_of(k)], parts.at[at], z1_s.at[k], z1_r.at[at], dev_p(k))
+
+    def part_in(k):
+        return remote(parts.at[k], parts.at[k], z1_s.at[pieces - k], z1_r.at[k], dev_p(k))
+
+    def sum_out(k):
+        mine = total.at[rows_of(0)]
+        return remote(mine, mine, z2_s.at[k], z2_r.at[pieces - k], dev_p(k))
+
+    def sum_in(k):
+        theirs = total.at[rows_of(k)]
+        return remote(theirs, theirs, z2_s.at[pieces - k], z2_r.at[k], dev_p(k))
+
+    over_y = remote(piece, from_y, yh_s, yh_r, (r + 2 - 4 * y_hi, f))
     pl.semaphore_wait(barrier, len(partners))
 
     def w_x(k):
@@ -143,6 +180,8 @@
     for k in (2, 1, 3):
         w_x(k).start()
     w_y[0][0]()
+    for k in range(1, pieces):
+        part_out(k).start()
 
     mask = mask_ref[...]
     n = mask.shape[1]
@@ -157,6 +196,7 @@
     pick[...] = jnp.where(
         lax.broadcasted_iota(jnp.int32, (ROWS, n), 0) == place, 1.0, 0.0
     ).astype(BF16)
+    loads[1].wait()
     kept = dot(pick[...], patch_ref[...])
     shifted = kept - jnp.mean(kept, axis=-1, keepdims=True)
     spread = jnp.mean(shifted * shifted, axis=-1, keepdims=True)
@@ -205,79 +245,41 @@
     c_x = along_x(cotb, cx_s, cx_r)
     a_x[0]()
 
-    def rows8(at, size):
-        return pl.ds(pl.multiple_of(at, 8), size)
-
-    pair1 = remote(delta_ref.at[rows8(128 * (1 - core), 128)], rec1, pc_s.at[0], pc_r.at[0], (r_core, f))
-    pair1.start()
-
     for k in (1, 3, 2):
         w_x_in(k).wait_recv()
         w_y[k][0]()
 
+    loads[2].wait()
+    owbuf[y, 0:56, :] = outw_ref[...]
+    owbuf[y, 56:64, :] = jnp.zeros((8, outw_ref.shape[1]), BF16)
+    loads[3].wait()
     cotb[x] = dot(pick[...], cot_ref[...]).astype(BF16)
-    pair1.wait_recv()
-    sum1[...] = delta_ref[rows8(128 * core, 128), :] + rec1[...]
-    pair2 = remote(sum1.at[rows8(64 * (1 - y_hi), 64)], rec2, pc_s.at[1], pc_r.at[1], (r_yhi, f))
-    pair2.start()
-
     a_x[1]()
-    w_y[0][1]()
     c_x[0]()
-    pair2.wait_recv()
-    sum2[...] = sum1[rows8(64 * y_hi, 64), :] + rec2[...]
-
-    def z_out(k):
-        to = lax.rem(z + k, nz)
-        return remote(sum2.at[rows8(8 * to, 8)], rec3.at[nz - k], z1_s.at[k], z1_r.at[nz - k], dev_z(k))
-
-    for k in range(1, nz):
-        z_out(k).start()
-    w_y[1][1]()
-    w_y[3][1]()
-
-    def z_in(k):
-        return remote(rec3.at[k], rec3.at[k], z1_s.at[nz - k], z1_r.at[k], dev_z(k))
-
-    mine = sum2[rows8(8 * z, 8), :]
-    for k in range(1, nz):
-        z_in(k).wait_recv()
-        mine = mine + rec3[k]
-    base = 128 * core + 64 * y_hi
-    total[rows8(base + 8 * z, 8), :] = mine
-
-    def z_back(k):
-        part = total.at[rows8(base + 8 * z, 8)]
-        return remote(part, part, z2_s.at[k], z2_r.at[nz - k], dev_z(k))
-
-    def z_back_in(k):
-        part = total.at[rows8(base + 8 * lax.rem(z + k, nz), 8)]
-        return remote(part, part, z2_s.at[nz - k], z2_r.at[k], dev_z(k))
-
-    for k in range(1, nz):
-        z_back(k).start()
-    w_y[2][1]()
+    mine = local[rows_of(0), :]
+    for k in range(1, pieces):
+        part_in(k).wait_recv()
+        mine = mine + parts[k]
+    piece[...] = mine
+    over_y.start()
+    for k in (0, 1):
+        w_y[k][1]()
+    over_y.wait_recv()
+    total[rows_of(0), :] = piece[...] + from_y[...]
+    for k in range(1, pieces):
+        sum_out(k).start()
+    for k in (3, 2):
+        w_y[k][1]()
     o_y[0]()
     c_x[1]()
-
-    for k in range(1, nz):
-        z_back_in(k).wait_recv()
-
-    def two_out(i, at, size, dev):
-        part = total.at[rows8(at, size)]
-        return remote(part, part, pc_s.at[i], pc_r.at[i], dev)
-
-    pair3 = two_out(2, base, 64, (r_yhi, f))
-    pair3.start()
-    two_out(2, 128 * core + 64 * (1 - y_hi), 64, (r_yhi, f)).wait_recv()
-    pair4 = two_out(3, 128 * core, 128, (r_core, f))
-    pair4.start()
-    two_out(3, 128 * (1 - core), 128, (r_core, f)).wait_recv()
-    average = total[...] * (1.0 / 32.0)
-    new_m = 0.9 * mom_ref[...] + average
+    for k in range(1, pieces):
+        sum_in(k).wait_recv()
+    loads[5].wait()
+    loads[6].wait()
+    average = total[...] / lax.axis_size("replica")
+    new_m = 0.9 * synced(mom_ref) + average
     newm_ref[...] = new_m
-    newp_ref[...] = par_ref[...] - 0.7 * (average + 0.9 * new_m)
-    o_y[1]()
+    newp_ref[...] = synced(par_ref) - 0.7 * (average + 0.9 * new_m)
 
     a_x[2]()
     for k in range(NX):
@@ -302,75 +304,124 @@
 
     lax.fori_loop(0, NX, attend, 0)
 
+    o_y[1]()
     o_y[2]()
-    def project(i, carry):
-        lo_send[i] = dot(att[i], owbuf[...].reshape(NY * 64, width)).astype(BF16)
-        return carry
-
-    lax.fori_loop(0, NX, project, 0)
-
-    def lo_out(k):
-        return remote(lo_send.at[at_x(k)], lo_recv.at[NX - k], lx_s.at[k], lx_r.at[NX - k], dev_x(k))
-
-    def lo_in(k):
-        return remote(lo_recv.at[k], lo_recv.at[k], lx_s.at[NX - k], lx_r.at[k], dev_x(k))
-
-    for k in (2, 1, 3):
-        lo_out(k).start()
+
+    def project(k):
+        lo_send[at_x(k)] = dot(att[at_x(k)], owbuf[...].reshape(NY * 64, width)).astype(BF16)
+
+    def lo(i, src, dst, to):
+        return remote(src, dst, lx_s.at[i], lx_r.at[i], dev_x(to))
+
+    right, left, over = at_x(1), at_x(3), at_x(2)
+    lo_far = [
+        lo(0, lo_send.at[over, low], lo_mid.at[0], 1), lo(1, lo_send.at[over, high], lo_mid.at[1], 3)
+    ]
+    lo_own = [
+        lo(2, lo_send.at[right, high], lo_recv.at[0, high], 1),
+        lo(3, lo_send.at[left, low], lo_recv.at[1, low], 3),
+    ]
+    lo_both = [
+        lo(4, lo_send.at[right, low], lo_recv.at[0, low], 1),
+        lo(5, lo_send.at[left, high], lo_recv.at[1, high], 3),
+    ]
+    project(2)
+    for c in lo_far:
+        c.start()
+    project(1)
+    lo_own[0].start()
+    project(3)
+    lo_own[1].start()
 
     c_x[2]()
     g_send[...] = dot(
         att[...].reshape(NX * ROWS, 256), cotb[...].reshape(NX * ROWS, width), (((0,), (0,)), ((), ()))
     ).astype(BF16).reshape(NY, 64, width)
 
-    def g_out(k):
+    def g(k):
         return remote(g_send.at[at_y(k)], g_recv.at[NY - k], gy_s.at[k], gy_r.at[NY - k], dev_y(at_y(k)))
 
     def g_in(k):
         return remote(g_recv.at[k], g_recv.at[k], gy_s.at[NY - k], gy_r.at[k], dev_y(at_y(k)))
 
-    for k in (2, 1, 3):
-        g_out(k).start()
+    def g_far(to, via):
+        return remote(g_send.at[to], g_mid, gm_s, gm_r, dev_y(via))
+
+    ends = (y == 0) | (y == NY - 1)
+    pl.when(y == 0)(lambda: g_far(3, 1).start())
+    pl.when(y == 3)(lambda: g_far(0, 2).start())
+
+    def near_y(k):
+        return jnp.abs(at_y(k) - y) < 2
+
+    for k in (1, 3):
+        pl.when(near_y(k))(lambda k=k: g(k).start())
+    pl.when(ends)(lambda: g(2).start())
+
+    lo_far[0].wait_recv()
+    lo_send[right, low] = (lo_send[right, low].astype(F32) + lo_mid[0].astype(F32)).astype(BF16)
+    lo_both[0].start()
+    lo_far[1].wait_recv()
+    lo_send[left, high] = (lo_send[left, high].astype(F32) + lo_mid[1].astype(F32)).astype(BF16)
+    lo_both[1].start()
+
+    def g_pass():
+        to = jnp.where(y == 1, 3, 0)
+        g_far(0, 2).wait_recv()
+        g_send[to] = (g_send[to].astype(F32) + g_mid[...].astype(F32)).astype(BF16)
+        g(2).start()
+
+    pl.when(jnp.logical_not(ends))(g_pass)
+    project(0)
 
     whole = g_send[y].astype(F32)
-    for k in (1, 2, 3):
-        g_in(k).wait_recv()
-        whole = whole + g_recv[k].astype(F32)
-    grad_ref[...] = whole[0:56, :]
-
-    result = lo_send[x].astype(F32)
-    for k in (1, 3, 2):
-        lo_in(k).wait_recv()
-        result = result + lo_recv[k].astype(F32)
+    g_in(2).wait_recv()
+    grad_ref[...] = (whole + g_recv[2].astype(F32))[0:56, :]
+    for k in (1, 3):
+
+        def add(k=k):
+            g_in(k).wait_recv()
+            grad_ref[...] += g_recv[k, 0:56].astype(F32)
+
+        pl.when(near_y(k))(add)
+
+    for i in (0, 1):
+        lo_own[i].wait_recv()
+    for i in (0, 1):
+        lo_both[i].wait_recv()
+    result = lo_send[x].astype(F32) + lo_recv[0].astype(F32) + lo_recv[1].astype(F32)
     out_ref[...] = dot(pick[...], result.astype(BF16), (((0,), (0,)), ((), ()))).astype(BF16)
 
     for k in (1, 2, 3):
         w_x(k).wait_send()
-        lo_out(k).wait_send()
-        g_out(k).wait_send()
+    for c in lo_far + lo_own + lo_both:
+        c.wait_send()
+    for k in range(1, pieces):
+        part_out(k).wait_send()
+        sum_out(k).wait_send()
+    over_y.wait_send()
+    for k in (1, 3):
+        pl.when(near_y(k))(lambda k=k: g(k).wait_send())
+    g(2).wait_send()
+    pl.when(ends)(lambda: g_far(0, 1).wait_send())
     for k in range(NX):
         w_y[k][3]()
     o_y[3]()
     a_x[3]()
     c_x[3]()
-    for c in (pair1, pair2, pair3, pair4):
-        c.wait_send()
-    for k in range(1, nz):
-        z_out(k).wait_send()
-        z_back(k).wait_send()
 
 
 def on_device(
     patch_rows, qkv_weight, out_weight, cotangent, keep_mask, outer_delta, momentum, global_params,
     fragment_index,
 ):
-    index = fragment_index[0]
-    delta = lax.dynamic_index_in_dim(outer_delta[0], index, 0, keepdims=False).reshape(256, 128)
-    old_m = lax.dynamic_index_in_dim(momentum, index, 0, keepdims=False).reshape(256, 128)
-    old_p = lax.dynamic_index_in_dim(global_params, index, 0, keepdims=False).reshape(256, 128)
+    def tiled(rows):
+        return rows.reshape(2, 256, 128).transpose(1, 0, 2)
+
+    pieces = lax.axis_size("replica") // 2
     width = patch_rows.shape[2]
-    nz = lax.axis_size("replica") // 4
     vmem = pl.BlockSpec(memory_space=pltpu.VMEM)
+    hbm = pl.BlockSpec(memory_space=pltpu.HBM)
     sem = pltpu.SemaphoreType.DMA
     shapes = [
         jax.ShapeDtypeStruct((256, width), BF16),
@@ -381,9 +432,21 @@
     out, grad, new_m, new_p = pl.pallas_call(
         kernel,
         out_shape=shapes,
-        in_specs=[vmem] * 8,
+        in_specs=[hbm] * 7 + [vmem, pl.BlockSpec(memory_space=pltpu.SMEM)],
         out_specs=[vmem] * 4,
         scratch_shapes=[
+            pltpu.VMEM((256, width), BF16),
+            pltpu.VMEM((112, 2688), BF16),
+            pltpu.VMEM((56, width), BF16),
+            pltpu.VMEM((256, width), BF16),
+            pltpu.VMEM((256, 2, 128), F32),
+            pltpu.VMEM((256, 2, 128), F32),
+            pltpu.VMEM((256, 2, 128), F32),
+            pltpu.VMEM((256, 128), F32),
+            pltpu.VMEM((16, 128), F32),
+            pltpu.VMEM((16, 128), F32),
+            pltpu.VMEM((pieces, 16, 128), F32),
+            pltpu.VMEM((256, 128), F32),
             pltpu.VMEM((ROWS, 256), BF16),
             pltpu.VMEM((NX, 112, 768), BF16),
             pltpu.VMEM((NX * NY, 112, 768), BF16),
@@ -393,27 +456,25 @@
             pltpu.VMEM((NX, ROWS, 768), BF16),
             pltpu.VMEM((NX, ROWS, 256), BF16),
             pltpu.VMEM((NX, ROWS, width), BF16),
-            pltpu.VMEM((NX, ROWS, width), BF16),
+            pltpu.VMEM((2, ROWS, width), BF16),
+            pltpu.VMEM((2, HALF, width), BF16),
             pltpu.VMEM((NY, 64, width), BF16),
             pltpu.VMEM((NY, 64, width), BF16),
-            pltpu.VMEM((128, 128), F32),
-            pltpu.VMEM((64, 128), F32),
-            pltpu.VMEM((128, 128), F32),
-            pltpu.VMEM((64, 128), F32),
-            pltpu.VMEM((nz, 8, 128), F32),
-            pltpu.VMEM((256, 128), F32),
+            pltpu.VMEM((64, width), BF16),
             sem((NX,)), sem((NX,)),
             sem((NX, NY)), sem((NX, NY)), sem((NX,)),
             sem((6,)), sem((6,)), sem((6,)), sem((6,)),
             sem((NY,)), sem((NY,)), sem,
-            sem((NX,)), sem((NX,)), sem((NY,)), sem((NY,)),
-            sem((4,)), sem((4,)), sem((nz,)), sem((nz,)), sem((nz,)), sem((nz,)),
+            sem((6,)), sem((6,)), sem((NY,)), sem((NY,)), sem, sem, sem((7,)),
+            sem((pieces,)), sem((pieces,)), sem((pieces,)), sem((pieces,)), sem, sem,
         ],
         compiler_params=pltpu.CompilerParams(
-            collective_id=0, has_side_effects=True, vmem_limit_bytes=48 * 1024 * 1024
+            collective_id=0, has_side_effects=True, vmem_limit_bytes=63 * 1024 * 1024
         ),
+        cost_estimate=pl.CostEstimate(flops=100_000_000_000, bytes_accessed=5_000_000, transcendentals=0),
     )(
-        patch_rows[0], qkv_weight[0], out_weight[0], cotangent[0], keep_mask, delta, old_m, old_p
+        patch_rows[0], qkv_weight[0], out_weight[0], cotangent[0], tiled(outer_delta[0]),
+        tiled(momentum), tiled(global_params), keep_mask, fragment_index,
     )
     return out[None], grad[None], new_m.reshape(-1), new_p.reshape(-1)
 

time: 125 us -> 107 us (0.86)
  Pallas kernels: 116 us -> 101 us
  local copies, waits for them, and re-layouts: 7.69 us -> 4.85 us
    pallas_call x1, Pallas kernels: 116 us -> 101 us  [on_device(): pl.pallas_call(kernel, out_shape=shapes, in_specs=[hbm] * 7 + [vmem, pl.B...]
    dynamic_slice x2 -> x0, local copies, waits for them, and re-layouts: 1.46 us -> none  [the longest x1 1.34 us: on_device(): lax.dynamic_index_in_dim(global_params, index, 0, keepdims=False)]
    unnamed x16 -> x10, local copies, waits for them, and re-layouts: 6.23 us -> 4.85 us
where the time goes in v2:
time: 107 us
  Pallas kernels  101 us (94%)
  local copies, waits for them, and re-layouts  4.85 us (5%)
  between operations  1.3 us (1%)
    pallas_call x1, Pallas kernels, on_device(): pl.pallas_call(kernel, out_shape=shapes, in_specs=[hbm] * 7 + [vmem, pl.B...  101 us
    unnamed x10, local copies, waits for them, and re-layouts  4.85 us

profile of v2, /device:TPU:56, one launch (start us, length us, event | category | flops | bytes accessed | tf_op | source)
XLA Modules:
  0.0 106.7 jit_solution(2336090942155559259)
XLA Ops:
  1.3 100.5 %shard_map.120 = (bf16[256,1792]{1,0:T(8,128)(2,1)}, f32[56,1792]{1,0:T(8,128)}, f32[256,128]{1,0:T(8,128)}, f32[256,128]{1,0:T(8,128)}) custom-call(bf16[256,1792]{1,0:T(8,128)(2,1)} %bitcast.21, bf16[112,2688]{1,0:T(8,128)(2,1)} %bitcast.23, bf16[56,1792]{1,0:T(8,128)(2,1)} %bitcast.27, bf16[256,1792]{1,0:T(8,128)(2,1)} %bitcast.22, ...), custom_call_target="tpu_custom_call" | custom-call | flops 99999997952 | bytes 5000000 | tf_op jit(solution)/shard_map/pallas_call | solution.py:432
  101.8 0.0 copy-start
  101.8 2.2 %copy.18 = bf16[1,256,1792]{2,1,0:T(8,128)(2,1)} copy(bf16[1,256,1792]{2,1,0:T(8,128)(2,1)} %bitcast.17) | data formatting | bytes 1835008
  104.0 0.0 copy-done
  104.0 0.0 copy-start.2
  104.0 0.7 copy.19
  104.8 0.3 copy-done.2
  105.1 0.0 copy-start.1
  105.1 0.7 copy.20
  105.7 0.3 copy-done.1
  106.0 0.7 copy.21
Async XLA Ops:
  101.8 2.2 %copy-start = (f32[56,1792]{1,0:T(8,128)S(1)}, f32[56,1792]{1,0:T(8,128)}, u32[]{:S(2)}) copy-start(f32[56,1792]{1,0:T(8,128)} %get-tuple-element.9) | copy-start | bytes 1204228
  104.0 1.0 copy-start.2
  105.1 1.0 copy-start.1

commit v3 on v2

--- a/solution.py
+++ b/solution.py
@@ -29,7 +29,7 @@
     out_ref, grad_ref, newm_ref, newp_ref,
     patch_ref, qkvw_ref, outw_ref, cot_ref, delta_ref, mom_ref, par_ref,
     local, piece, from_y, parts, total,
-    pick, wpack, wbuf, act, cotb, owbuf, qkv, att, lo_send, lo_recv, lo_mid, g_send, g_recv, g_mid,
+    pick, wide, wpack, wbuf, whole_w, act, cotb, oraw, owbuf, qkv, att, lo_send, lo_recv, lo_mid, g_send, g_recv, g_mid,
     wx_s, wx_r, wy_s, wy_r, wf_s, ax_s, ax_r, cx_s, cx_r, oy_s, oy_r, of_s,
     lx_s, lx_r, gy_s, gy_r, gm_s, gm_r, in_s, z1_s, z1_r, z2_s, z2_r, yh_s, yh_r,
 ):
@@ -79,16 +79,40 @@
     for dev in partners:
         pl.semaphore_signal(barrier, inc=1, device_id=dev, device_id_type=MESH)
 
+    def one_hot(shape, of):
+        row = lax.broadcasted_iota(jnp.int32, shape, 0)
+        return jnp.where(of(row, lax.broadcasted_iota(jnp.int32, shape, 1)), 1.0, 0.0).astype(BF16)
+
     loads[0].wait()
     for k in range(NX):
         start = min(224 * k // 128, 4) * 128
-        row = lax.broadcasted_iota(jnp.int32, (384, 256), 0)
-        lane = lax.broadcasted_iota(jnp.int32, (384, 256), 1)
-        wanted = 224 * k - start + 56 * (lane // 64) + lane % 64
-        chosen = jnp.where((row == wanted) & (lane % 64 < 56), 1.0, 0.0).astype(BF16)
+        shift = 224 * k - start
+        chosen = one_hot(
+            (384, 256), lambda i, j: (i == shift + 112 * (j // 128) + j % 128) & (j % 128 < 112)
+        )
         for t in range(3):
             cols = qkvw_ref[:, 896 * t + start : 896 * t + start + 384]
-            wpack[k, :, 256 * t : 256 * t + 256] = dot(cols, chosen).astype(BF16)
+            wide[112 * k : 112 * k + 112, 256 * t : 256 * t + 256] = dot(cols, chosen).astype(BF16)
+    spread6 = one_hot(
+        (128, 768),
+        lambda i, j: ((j < 640) & (j % 128 >= 112) & (i == 16 * (j // 128) + j % 128 - 112))
+        | ((j >= 640) & (i == 80 + j % 32)),
+    )
+    filled = dot(wide[:, 640:768], spread6)
+    fold = one_hot((32, 112), lambda i, j: (i < 28) & (j % 28 == i))
+    group = (
+        lax.broadcasted_iota(jnp.int32, (112, 128), 0) // 28
+        == lax.broadcasted_iota(jnp.int32, (112, 128), 1) // 32
+    )
+    for k in range(NX):
+        rows = slice(112 * k, 112 * k + 112)
+        for t in range(5):
+            lanes = slice(128 * t, 128 * t + 128)
+            wpack[k, 112 * t : 112 * t + 112, :] = (
+                wide[rows, lanes].astype(F32) + filled[rows, lanes]
+            ).astype(BF16)
+        rest = jnp.where(group, filled[rows, 640:768], 0.0).astype(BF16)
+        wpack[k, 560:592, :] = dot(fold, rest).astype(BF16)
     wbuf[f] = wpack[x]
 
     def synced(ref):
@@ -175,7 +199,7 @@
         )
         for k in range(NX)
     ]
-    o_y = along_y(lambda yy: owbuf.at[yy], lambda j: oy_s.at[j], lambda yy: oy_r.at[yy], of_s)
+    o_y = along_y(lambda yy: oraw.at[yy], lambda j: oy_s.at[j], lambda yy: oy_r.at[yy], of_s)
 
     for k in (2, 1, 3):
         w_x(k).start()
@@ -250,8 +274,8 @@
         w_y[k][0]()
 
     loads[2].wait()
-    owbuf[y, 0:56, :] = outw_ref[...]
-    owbuf[y, 56:64, :] = jnp.zeros((8, outw_ref.shape[1]), BF16)
+    oraw[y, 0:56, :] = outw_ref[:, 0:896]
+    oraw[y, 56:112, :] = outw_ref[:, 896:1792]
     loads[3].wait()
     cotb[x] = dot(pick[...], cot_ref[...]).astype(BF16)
     a_x[1]()
@@ -282,18 +306,37 @@
     newp_ref[...] = synced(par_ref) - 0.7 * (average + 0.9 * new_m)
 
     a_x[2]()
-    for k in range(NX):
+    width = act.shape[2]
+    unfold = one_hot((112, 32), lambda i, j: i % 28 == j)
+    back = one_hot((128, 128), lambda i, j: (j < 32) & (i % 32 == j))
+
+    for k in (0, 1, 3, 2):
         w_y[k][2]()
-    width = act.shape[2]
+
+        def unpack(j, carry, k=k):
+            at = at_x(k) * NY + j
+            for t in range(5):
+                whole_w[at, :, 128 * t : 128 * t + 128] = wbuf[at, 112 * t : 112 * t + 112, :]
+            rest = jnp.where(group, dot(unfold, wbuf[at, 560:592, :]), 0.0).astype(BF16)
+            whole_w[at, :, 640:768] = dot(rest, back).astype(BF16)
+            return carry
+
+        lax.fori_loop(0, NY, unpack, 0)
     qkv[...] = dot(
-        act[...].reshape(NX * ROWS, width), wbuf[...].reshape(width, 768)
+        act[...].reshape(NX * ROWS, width), whole_w[...].reshape(width, 768)
     ).astype(BF16).reshape(NX, ROWS, 768)
+    sixth = one_hot(
+        (768, 128),
+        lambda i, j: ((i < 640) & (i % 128 >= 112) & (j == 16 * (i // 128) + i % 128 - 112))
+        | ((i >= 640) & (i < 672) & (j == i - 560)),
+    )
 
     def attend(i, carry):
         for h in range(2):
             q = qkv[i, :, 128 * h : 128 * h + 128]
+            q = jnp.where(lax.broadcasted_iota(jnp.int32, (ROWS, 128), 1) < HSZ, q, jnp.zeros_like(q))
             key = qkv[i, :, 256 + 128 * h : 384 + 128 * h]
-            val = qkv[i, :, 512 + 128 * h : 640 + 128 * h]
+            val = qkv[i, :, 512:640] if h == 0 else dot(qkv[i], sixth).astype(BF16)
             scores = dot(q, key, (((1,), (1,)), ((), ()))) * (1.0 / math.sqrt(HSZ))
             col = lax.broadcasted_iota(jnp.int32, (ROWS, ROWS), 1)
             scores = jnp.where(col < KEEP, scores, -1e30)
@@ -306,9 +349,15 @@
 
     o_y[1]()
     o_y[2]()
+    for j in range(NY):
+        rows = slice(128 * (j // 2) + 56 * (j % 2), 128 * (j // 2) + 56 * (j % 2) + 56)
+        owbuf[rows, 0:896] = oraw[j, 0:56, :]
+        owbuf[rows, 896:1792] = oraw[j, 56:112, :]
+    for h in range(2):
+        owbuf[128 * h + 112 : 128 * h + 128, :] = jnp.zeros((16, width), BF16)
 
     def project(k):
-        lo_send[at_x(k)] = dot(att[at_x(k)], owbuf[...].reshape(NY * 64, width)).astype(BF16)
+        lo_send[at_x(k)] = dot(att[at_x(k)], owbuf[...]).astype(BF16)
 
     def lo(i, src, dst, to):
         return remote(src, dst, lx_s.at[i], lx_r.at[i], dev_x(to))
@@ -334,9 +383,13 @@
     lo_own[1].start()
 
     c_x[2]()
-    g_send[...] = dot(
+    terms = dot(
         att[...].reshape(NX * ROWS, 256), cotb[...].reshape(NX * ROWS, width), (((0,), (0,)), ((), ()))
-    ).astype(BF16).reshape(NY, 64, width)
+    ).astype(BF16)
+    for j in range(NY):
+        rows = slice(128 * (j // 2) + 56 * (j % 2), 128 * (j // 2) + 56 * (j % 2) + 56)
+        g_send[j, 0:56, :] = terms[rows, 0:896]
+        g_send[j, 56:112, :] = terms[rows, 896:1792]
 
     def g(k):
         return remote(g_send.at[at_y(k)], g_recv.at[NY - k], gy_s.at[k], gy_r.at[NY - k], dev_y(at_y(k)))
@@ -376,12 +429,15 @@
 
     whole = g_send[y].astype(F32)
     g_in(2).wait_recv()
-    grad_ref[...] = (whole + g_recv[2].astype(F32))[0:56, :]
+    whole = whole + g_recv[2].astype(F32)
+    grad_ref[:, 0:896] = whole[0:56, :]
+    grad_ref[:, 896:1792] = whole[56:112, :]
     for k in (1, 3):
 
         def add(k=k):
             g_in(k).wait_recv()
-            grad_ref[...] += g_recv[k, 0:56].astype(F32)
+            grad_ref[:, 0:896] += g_recv[k, 0:56].astype(F32)
+            grad_ref[:, 896:1792] += g_recv[k, 56:112].astype(F32)
 
         pl.when(near_y(k))(add)
 
@@ -411,6 +467,23 @@
     c_x[3]()
 
 
+def hand_out(out_in, grad_in, newm_in, newp_in, out_ref, grad_ref, newm_ref, newp_ref, out_v, grad_v, m_v, p_v, sems):
+    steps = [(out_in, out_v, out_ref, pl.ds(64 * i, 64)) for i in range(4)]
+    steps += [(grad_in, grad_v, grad_ref, pl.ds(0, 56))]
+    steps += [(newm_in, m_v, newm_ref, pl.ds(0, 256)), (newp_in, p_v, newp_ref, pl.ds(0, 256))]
+    loads, stores = [], []
+    for i, (src, held, dst, rows) in enumerate(steps):
+        loads.append(pltpu.make_async_copy(src.at[rows], held.at[rows], sems.at[0, i]))
+        stores.append(pltpu.make_async_copy(held.at[rows], dst.at[rows], sems.at[1, i]))
+    for c in loads:
+        c.start()
+    for load, store in zip(loads, stores):
+        load.wait()
+        store.start()
+    for c in stores:
+        c.wait()
+
+
 def on_device(
     patch_rows, qkv_weight, out_weight, cotangent, keep_mask, outer_delta, momentum, global_params,
     fragment_index,
@@ -429,7 +502,7 @@
         jax.ShapeDtypeStruct((256, 128), F32),
         jax.ShapeDtypeStruct((256, 128), F32),
     ]
-    out, grad, new_m, new_p = pl.pallas_call(
+    results = pl.pallas_call(
         kernel,
         out_shape=shapes,
         in_specs=[hbm] * 7 + [vmem, pl.BlockSpec(memory_space=pltpu.SMEM)],
@@ -448,19 +521,22 @@
             pltpu.VMEM((pieces, 16, 128), F32),
             pltpu.VMEM((256, 128), F32),
             pltpu.VMEM((ROWS, 256), BF16),
-            pltpu.VMEM((NX, 112, 768), BF16),
+            pltpu.VMEM((NX * 112, 768), BF16),
+            pltpu.VMEM((NX, 592, 128), BF16),
+            pltpu.VMEM((NX * NY, 592, 128), BF16),
             pltpu.VMEM((NX * NY, 112, 768), BF16),
             pltpu.VMEM((NX, ROWS, width), BF16),
             pltpu.VMEM((NX, ROWS, width), BF16),
-            pltpu.VMEM((NY, 64, width), BF16),
+            pltpu.VMEM((NY, 112, 896), BF16),
+            pltpu.VMEM((256, width), BF16),
             pltpu.VMEM((NX, ROWS, 768), BF16),
             pltpu.VMEM((NX, ROWS, 256), BF16),
             pltpu.VMEM((NX, ROWS, width), BF16),
             pltpu.VMEM((2, ROWS, width), BF16),
             pltpu.VMEM((2, HALF, width), BF16),
-            pltpu.VMEM((NY, 64, width), BF16),
-            pltpu.VMEM((NY, 64, width), BF16),
-            pltpu.VMEM((64, width), BF16),
+            pltpu.VMEM((NY, 112, 896), BF16),
+            pltpu.VMEM((NY, 112, 896), BF16),
+            pltpu.VMEM((112, 896), BF16),
             sem((NX,)), sem((NX,)),
             sem((NX, NY)), sem((NX, NY)), sem((NX,)),
             sem((6,)), sem((6,)), sem((6,)), sem((6,)),
@@ -476,6 +552,14 @@
         patch_rows[0], qkv_weight[0], out_weight[0], cotangent[0], tiled(outer_delta[0]),
         tiled(momentum), tiled(global_params), keep_mask, fragment_index,
     )
+    out, grad, new_m, new_p = pl.pallas_call(
+        hand_out,
+        out_shape=shapes,
+        in_specs=[hbm] * 4,
+        out_specs=[hbm] * 4,
+        scratch_shapes=[pltpu.VMEM(a.shape, a.dtype) for a in shapes] + [sem((2, 7))],
+        compiler_params=pltpu.CompilerParams(vmem_limit_bytes=63 * 1024 * 1024),
+    )(*results)
     return out[None], grad[None], new_m.reshape(-1), new_p.reshape(-1)
 
 

time: 107 us -> 98.6 us (0.921)
  local copies, waits for them, and re-layouts: 4.85 us -> 0 us
  Pallas kernels: 101 us -> 97.2 us
    pallas_call x1, Pallas kernels: 101 us -> 94.8 us  [on_device(): pl.pallas_call(kernel, out_shape=shapes, in_specs=[hbm] * 7 + [vmem, pl.B...]
    unnamed x10 -> x0, local copies, waits for them, and re-layouts: 4.85 us -> none
    pallas_call x0 -> x1, Pallas kernels: none -> 2.36 us  [on_device(): pl.pallas_call(hand_out, out_shape=shapes, in_specs=[hbm] * 4, out_specs=...]
where the time goes in v3:
time: 98.6 us; the launch traced here: 98.5 us
  Pallas kernels  97.2 us (99%)
  between operations  1.29 us (1%)
    pallas_call x1, Pallas kernels, on_device(): pl.pallas_call(kernel, out_shape=shapes, in_specs=[hbm] * 7 + [vmem, pl.B...  94.8 us
    pallas_call x1, Pallas kernels, on_device(): pl.pallas_call(hand_out, out_shape=shapes, in_specs=[hbm] * 4, out_specs=...  2.36 us

profile of v3, /device:TPU:56, one launch (start us, length us, event | category | flops | bytes accessed | tf_op | source)
XLA Modules:
  0.0 98.5 jit_solution(15954290340110303885)
XLA Ops:
  1.3 94.8 %shard_map.120 = (bf16[256,1792]{1,0:T(8,128)(2,1)}, f32[56,1792]{1,0:T(8,128)}, f32[256,128]{1,0:T(8,128)}, f32[256,128]{1,0:T(8,128)}) custom-call(bf16[256,1792]{1,0:T(8,128)(2,1)} %bitcast.17, bf16[112,2688]{1,0:T(8,128)(2,1)} %bitcast.20, bf16[56,1792]{1,0:T(8,128)(2,1)} %bitcast.25, bf16[256,1792]{1,0:T(8,128)(2,1)} %bitcast.18, ...), custom_call_target="tpu_custom_call" | custom-call | flops 99999997952 | bytes 5000000 | tf_op jit(solution)/shard_map/pallas_call | solution.py:505
  96.1 2.4 %shard_map.121 = (bf16[256,1792]{1,0:T(8,128)(2,1)}, f32[56,1792]{1,0:T(8,128)}, f32[256,128]{1,0:T(8,128)}, f32[256,128]{1,0:T(8,128)}) custom-call(bf16[256,1792]{1,0:T(8,128)(2,1)} %get-tuple-element.12.out_in, f32[56,1792]{1,0:T(8,128)} %get-tuple-element.13.grad_in, f32[256,128]{1,0:T(8,128)} %get-tuple-element.14.newm_in, ...), custom_call_target="tpu_custom_call" | custom-call | tf_op jit(solution)/shard_map/pallas_call | solution.py:555

commit v4 on v3

--- a/solution.py
+++ b/solution.py
@@ -31,7 +31,7 @@
     local, piece, from_y, parts, total,
     pick, wide, wpack, wbuf, whole_w, act, cotb, oraw, owbuf, qkv, att, lo_send, lo_recv, lo_mid, g_send, g_recv, g_mid,
     wx_s, wx_r, wy_s, wy_r, wf_s, ax_s, ax_r, cx_s, cx_r, oy_s, oy_r, of_s,
-    lx_s, lx_r, gy_s, gy_r, gm_s, gm_r, in_s, z1_s, z1_r, z2_s, z2_r, yh_s, yh_r,
+    lx_s, lx_r, gy_s, gy_r, gm_s, gm_r, in_s, z1_s, z1_r, z2_s, z2_r, yh_s, yh_r, below, above,
 ):
     r = lax.axis_index("replica")
     f = lax.axis_index("fsdp")
@@ -39,6 +39,7 @@
     pieces = lax.axis_size("replica") // 2
     own = r // 4 * 2 + lax.rem(r, 2)
     y_hi = lax.rem(r // 2, 2)
+    z, nz = r // 4, lax.axis_size("replica") // 4
 
     loads = [
         pltpu.make_async_copy(src, dst, in_s.at[i])
@@ -75,9 +76,28 @@
 
     barrier = pltpu.get_barrier_semaphore()
     partners = [dev_x(k) for k in (1, 2, 3)] + [dev_y(at_y(k)) for k in (1, 2, 3)]
-    partners += [(r + 2 - 4 * y_hi, f)] + [dev_p(k) for k in range(1, pieces)]
+    partners += [(r + 2 - 4 * y_hi, f), (r + 1 - 2 * lax.rem(r, 2), f)]
     for dev in partners:
         pl.semaphore_signal(barrier, inc=1, device_id=dev, device_id_type=MESH)
+
+    def tell(sem, dev):
+        pl.semaphore_signal(sem, inc=1, device_id=dev, device_id_type=MESH)
+
+    pl.when(z > 0)(lambda: tell(barrier, (r - 4, f)))
+    pl.when(z < nz - 1)(lambda: tell(barrier, (r + 4, f)))
+
+    def from_below():
+        pl.when(z > 0)(lambda: pl.semaphore_wait(below, 1))
+        pl.when(z < nz - 1)(lambda: tell(below, (r + 4, f)))
+
+    def from_above(p):
+        def step():
+            if p > 0:
+                pl.semaphore_wait(above, 1)
+            if p < nz - 1:
+                tell(above, (r - 4, f))
+
+        pl.when(z == nz - 1 - p)(step)
 
     def one_hot(shape, of):
         row = lax.broadcasted_iota(jnp.int32, shape, 0)
@@ -118,8 +138,6 @@
     def synced(ref):
         return jnp.where(jnp.full((256, 128), index_ref[0], jnp.int32) == 0, ref[:, 0, :], ref[:, 1, :])
 
-    loads[4].wait()
-    local[...] = synced(delta_ref)
 
     def rows_of(k):
         return pl.ds(pl.multiple_of(16 * lax.rem(own + k, pieces), 16), 16)
@@ -140,7 +158,10 @@
         return remote(theirs, theirs, z2_s.at[pieces - k], z2_r.at[k], dev_p(k))
 
     over_y = remote(piece, from_y, yh_s, yh_r, (r + 2 - 4 * y_hi, f))
-    pl.semaphore_wait(barrier, len(partners))
+    beside = jnp.where((z > 0) & (z < nz - 1), 2, 1)
+    pl.semaphore_wait(barrier, len(partners) + beside)
+    from_below()
+    from_above(0)
 
     def w_x(k):
         return remote(wpack.at[at_x(k)], wbuf.at[f], wx_s.at[k], wx_r.at[NX - k], dev_x(k))
@@ -204,8 +225,7 @@
     for k in (2, 1, 3):
         w_x(k).start()
     w_y[0][0]()
-    for k in range(1, pieces):
-        part_out(k).start()
+    from_above(1)
 
     mask = mask_ref[...]
     n = mask.shape[1]
@@ -268,42 +288,44 @@
     a_x = along_x(act, ax_s, ax_r)
     c_x = along_x(cotb, cx_s, cx_r)
     a_x[0]()
-
-    for k in (1, 3, 2):
+    from_above(2)
+
+    for p, k in enumerate((1, 3, 2)):
         w_x_in(k).wait_recv()
         w_y[k][0]()
+        from_above(3 + p)
 
     loads[2].wait()
     oraw[y, 0:56, :] = outw_ref[:, 0:896]
     oraw[y, 56:112, :] = outw_ref[:, 896:1792]
     loads[3].wait()
     cotb[x] = dot(pick[...], cot_ref[...]).astype(BF16)
+    loads[4].wait()
+    local[...] = synced(delta_ref)
     a_x[1]()
     c_x[0]()
+    from_above(6)
+    w_y[0][1]()
+    for p in range(7, nz):
+        from_above(p)
+    for k in range(1, pieces):
+        part_out(k).start()
+    for k in (1, 3):
+        w_y[k][1]()
+    o_y[0]()
     mine = local[rows_of(0), :]
     for k in range(1, pieces):
         part_in(k).wait_recv()
         mine = mine + parts[k]
     piece[...] = mine
     over_y.start()
-    for k in (0, 1):
-        w_y[k][1]()
+    w_y[2][1]()
+    c_x[1]()
     over_y.wait_recv()
     total[rows_of(0), :] = piece[...] + from_y[...]
     for k in range(1, pieces):
         sum_out(k).start()
-    for k in (3, 2):
-        w_y[k][1]()
-    o_y[0]()
-    c_x[1]()
-    for k in range(1, pieces):
-        sum_in(k).wait_recv()
-    loads[5].wait()
-    loads[6].wait()
-    average = total[...] / lax.axis_size("replica")
-    new_m = 0.9 * synced(mom_ref) + average
-    newm_ref[...] = new_m
-    newp_ref[...] = synced(par_ref) - 0.7 * (average + 0.9 * new_m)
+    o_y[1]()
 
     a_x[2]()
     width = act.shape[2]
@@ -331,7 +353,7 @@
         | ((i >= 640) & (i < 672) & (j == i - 560)),
     )
 
-    def attend(i, carry):
+    def attend(i):
         for h in range(2):
             q = qkv[i, :, 128 * h : 128 * h + 128]
             q = jnp.where(lax.broadcasted_iota(jnp.int32, (ROWS, 128), 1) < HSZ, q, jnp.zeros_like(q))
@@ -343,11 +365,7 @@
             expo = jnp.exp(scores - jnp.max(scores, axis=-1, keepdims=True))
             probs = (expo / jnp.sum(expo, axis=-1, keepdims=True)).astype(BF16)
             att[i, :, 128 * h : 128 * h + 128] = dot(probs, val).astype(BF16)
-        return carry
-
-    lax.fori_loop(0, NX, attend, 0)
-
-    o_y[1]()
+
     o_y[2]()
     for j in range(NY):
         rows = slice(128 * (j // 2) + 56 * (j % 2), 128 * (j // 2) + 56 * (j % 2) + 56)
@@ -374,13 +392,17 @@
         lo(4, lo_send.at[right, low], lo_recv.at[0, low], 1),
         lo(5, lo_send.at[left, high], lo_recv.at[1, high], 3),
     ]
+    attend(over)
     project(2)
     for c in lo_far:
         c.start()
+    attend(right)
     project(1)
     lo_own[0].start()
+    attend(left)
     project(3)
     lo_own[1].start()
+    attend(x)
 
     c_x[2]()
     terms = dot(
@@ -426,6 +448,15 @@
 
     pl.when(jnp.logical_not(ends))(g_pass)
     project(0)
+
+    for k in range(1, pieces):
+        sum_in(k).wait_recv()
+    loads[5].wait()
+    loads[6].wait()
+    average = total[...] / lax.axis_size("replica")
+    new_m = 0.9 * synced(mom_ref) + average
+    newm_ref[...] = new_m
+    newp_ref[...] = synced(par_ref) - 0.7 * (average + 0.9 * new_m)
 
     whole = g_send[y].astype(F32)
     g_in(2).wait_recv()
@@ -543,6 +574,7 @@
             sem((NY,)), sem((NY,)), sem,
             sem((6,)), sem((6,)), sem((NY,)), sem((NY,)), sem, sem, sem((7,)),
             sem((pieces,)), sem((pieces,)), sem((pieces,)), sem((pieces,)), sem, sem,
+            pltpu.SemaphoreType.REGULAR, pltpu.SemaphoreType.REGULAR,
         ],
         compiler_params=pltpu.CompilerParams(
             collective_id=0, has_side_effects=True, vmem_limit_bytes=63 * 1024 * 1024

time: 98.6 us -> 93.3 us (0.946)
  the two profiles are of different devices: /device:TPU:56 before, /device:TPU:130 now
where the time goes in v4:
time: 93.3 us; the launch traced here: 93.1 us
  Pallas kernels  91.8 us (98%)
  between operations  1.29 us (1%)
    pallas_call x1, Pallas kernels, on_device(): pl.pallas_call(kernel, out_shape=shapes, in_specs=[hbm] * 7 + [vmem, pl.B...  89.4 us
    pallas_call x1, Pallas kernels, on_device(): pl.pallas_call(hand_out, out_shape=shapes, in_specs=[hbm] * 4, out_specs=...  2.36 us

profile of v4, /device:TPU:130, one launch (start us, length us, event | category | flops | bytes accessed | tf_op | source)
XLA Modules:
  0.0 93.1 jit_solution(402886062283080025)
XLA Ops:
  1.3 89.4 %shard_map.120 = (bf16[256,1792]{1,0:T(8,128)(2,1)}, f32[56,1792]{1,0:T(8,128)}, f32[256,128]{1,0:T(8,128)}, f32[256,128]{1,0:T(8,128)}) custom-call(bf16[256,1792]{1,0:T(8,128)(2,1)} %bitcast.17, bf16[112,2688]{1,0:T(8,128)(2,1)} %bitcast.20, bf16[56,1792]{1,0:T(8,128)(2,1)} %bitcast.25, bf16[256,1792]{1,0:T(8,128)(2,1)} %bitcast.18, ...), custom_call_target="tpu_custom_call" | custom-call | flops 99999997952 | bytes 5000000 | tf_op jit(solution)/shard_map/pallas_call | solution.py:536
  90.7 2.4 %shard_map.121 = (bf16[256,1792]{1,0:T(8,128)(2,1)}, f32[56,1792]{1,0:T(8,128)}, f32[256,128]{1,0:T(8,128)}, f32[256,128]{1,0:T(8,128)}) custom-call(bf16[256,1792]{1,0:T(8,128)(2,1)} %get-tuple-element.12.out_in, f32[56,1792]{1,0:T(8,128)} %get-tuple-element.13.grad_in, f32[256,128]{1,0:T(8,128)} %get-tuple-element.14.newm_in, ...), custom_call_target="tpu_custom_call" | custom-call | tf_op jit(solution)/shard_map/pallas_call | solution.py:587

commit v5 on v4

--- a/solution.py
+++ b/solution.py
@@ -30,7 +30,7 @@
     patch_ref, qkvw_ref, outw_ref, cot_ref, delta_ref, mom_ref, par_ref,
     local, piece, from_y, parts, total,
     pick, wide, wpack, wbuf, whole_w, act, cotb, oraw, owbuf, qkv, att, lo_send, lo_recv, lo_mid, g_send, g_recv, g_mid,
-    wx_s, wx_r, wy_s, wy_r, wf_s, ax_s, ax_r, cx_s, cx_r, oy_s, oy_r, of_s,
+    wx_s, wx_r, wy_s, wy_r, ax_s, ax_r, cx_s, cx_r, oy_s, oy_r,
     lx_s, lx_r, gy_s, gy_r, gm_s, gm_r, in_s, z1_s, z1_r, z2_s, z2_r, yh_s, yh_r, below, above,
 ):
     r = lax.axis_index("replica")
@@ -170,44 +170,51 @@
         slot = wbuf.at[at_x(k) * NY + y]
         return remote(slot, slot, wx_s.at[NX - k], wx_r.at[k], dev_x(k))
 
-    def along_y(buf, send, recv, fwd):
-        def out(k):
-            to = at_y(k)
-            return remote(buf(y), buf(y), send(k), recv(y), dev_y(to))
-
-        def near(k):
-            return jnp.abs(at_y(k) - y) < 3
+    def along_y(buf, send, recv):
+        def down(src, i):
+            return remote(buf(src), buf(src), send(i), recv(src), dev_y(y - 1))
+
+        def up(src, i):
+            return remote(buf(src), buf(src), send(i), recv(src), dev_y(y + 1))
+
+        def can_down(d):
+            return (y > 0) & (y + d < NY)
+
+        def can_up(d):
+            return (y < NY - 1) & (y >= d)
 
         def start():
-            for k in (1, 3, 2):
-                pl.when(near(k))(lambda k=k: out(k).start())
-
-        def forward():
-            def from_low():
-                remote(buf(0), buf(0), fwd, recv(0), dev_y(3)).wait_recv()
-                remote(buf(0), buf(0), fwd, recv(0), dev_y(3)).start()
-
-            def from_high():
-                remote(buf(3), buf(3), fwd, recv(3), dev_y(0)).wait_recv()
-                remote(buf(3), buf(3), fwd, recv(3), dev_y(0)).start()
-
-            pl.when(y == 2)(from_low)
-            pl.when(y == 1)(from_high)
+            pl.when(can_down(0))(lambda: down(y, 0).start())
+            pl.when(can_up(0))(lambda: up(y, 1).start())
+
+        def forward(d):
+            def pass_down():
+                down(y + d, 2 * d).wait_recv()
+                down(y + d, 2 * d).start()
+
+            def pass_up():
+                up(y - d, 2 * d + 1).wait_recv()
+                up(y - d, 2 * d + 1).start()
+
+            pl.when(can_down(d))(pass_down)
+            pl.when(can_up(d))(pass_up)
 
         def finish():
-            for k in (1, 2, 3):
-                src = at_y(k)
-                done = ((y == 2) & (src == 0)) | ((y == 1) & (src == 3))
-                pl.when(jnp.logical_not(done))(
-                    lambda src=src: remote(buf(src), buf(src), fwd, recv(src), dev_y(src)).wait_recv()
-                )
+            def low_end():
+                for src in (1, 2, 3):
+                    up(src, 0).wait_recv()
+
+            def high_end():
+                for src in (2, 1, 0):
+                    down(src, 0).wait_recv()
+
+            pl.when(y == 0)(low_end)
+            pl.when(y == NY - 1)(high_end)
 
         def drain():
-            for k in (1, 3, 2):
-                pl.when(near(k))(lambda k=k: out(k).wait_send())
-            pl.when((y == 1) | (y == 2))(
-                lambda: remote(buf(y), buf(y), fwd, recv(y), dev_y(at_y(1))).wait_send()
-            )
+            for d in range(3):
+                pl.when(can_down(d))(lambda d=d: down(y, 2 * d).wait_send())
+                pl.when(can_up(d))(lambda d=d: up(y, 2 * d + 1).wait_send())
 
         return start, forward, finish, drain
 
@@ -216,11 +223,10 @@
             lambda yy, k=k: wbuf.at[at_x(k) * NY + yy],
             lambda j, k=k: wy_s.at[k, j],
             lambda yy, k=k: wy_r.at[k, yy],
-            wf_s.at[k],
         )
         for k in range(NX)
     ]
-    o_y = along_y(lambda yy: oraw.at[yy], lambda j: oy_s.at[j], lambda yy: oy_r.at[yy], of_s)
+    o_y = along_y(lambda yy: oraw.at[yy], lambda j: oy_s.at[j], lambda yy: oy_r.at[yy])
 
     for k in (2, 1, 3):
         w_x(k).start()
@@ -290,11 +296,15 @@
     a_x[0]()
     from_above(2)
 
-    for p, k in enumerate((1, 3, 2)):
+    for p, k in enumerate((1, 3)):
         w_x_in(k).wait_recv()
         w_y[k][0]()
         from_above(3 + p)
-
+    w_y[0][1](1)
+    w_x_in(2).wait_recv()
+    w_y[2][0]()
+    from_above(5)
+    w_y[1][1](1)
     loads[2].wait()
     oraw[y, 0:56, :] = outw_ref[:, 0:896]
     oraw[y, 56:112, :] = outw_ref[:, 896:1792]
@@ -302,16 +312,18 @@
     cotb[x] = dot(pick[...], cot_ref[...]).astype(BF16)
     loads[4].wait()
     local[...] = synced(delta_ref)
+    w_y[3][1](1)
+    from_above(6)
+    w_y[2][1](1)
     a_x[1]()
     c_x[0]()
-    from_above(6)
-    w_y[0][1]()
     for p in range(7, nz):
         from_above(p)
     for k in range(1, pieces):
         part_out(k).start()
-    for k in (1, 3):
-        w_y[k][1]()
+    for k in (0, 1, 3):
+        w_y[k][1](2)
+    w_y[2][1](2)
     o_y[0]()
     mine = local[rows_of(0), :]
     for k in range(1, pieces):
@@ -319,13 +331,7 @@
         mine = mine + parts[k]
     piece[...] = mine
     over_y.start()
-    w_y[2][1]()
     c_x[1]()
-    over_y.wait_recv()
-    total[rows_of(0), :] = piece[...] + from_y[...]
-    for k in range(1, pieces):
-        sum_out(k).start()
-    o_y[1]()
 
     a_x[2]()
     width = act.shape[2]
@@ -347,6 +353,11 @@
     qkv[...] = dot(
         act[...].reshape(NX * ROWS, width), whole_w[...].reshape(width, 768)
     ).astype(BF16).reshape(NX, ROWS, 768)
+    o_y[1](1)
+    over_y.wait_recv()
+    total[rows_of(0), :] = piece[...] + from_y[...]
+    for k in range(1, pieces):
+        sum_out(k).start()
     sixth = one_hot(
         (768, 128),
         lambda i, j: ((i < 640) & (i % 128 >= 112) & (j == 16 * (i // 128) + i % 128 - 112))
@@ -366,6 +377,20 @@
             probs = (expo / jnp.sum(expo, axis=-1, keepdims=True)).astype(BF16)
             att[i, :, 128 * h : 128 * h + 128] = dot(probs, val).astype(BF16)
 
+    for k in (0, 1):
+        attend(at_x(k))
+    o_y[1](2)
+    for k in (2, 3):
+        attend(at_x(k))
+    c_x[2]()
+    terms = dot(
+        att[...].reshape(NX * ROWS, 256), cotb[...].reshape(NX * ROWS, width), (((0,), (0,)), ((), ()))
+    ).astype(BF16)
+    for j in range(NY):
+        rows = slice(128 * (j // 2) + 56 * (j % 2), 128 * (j // 2) + 56 * (j % 2) + 56)
+        g_send[j, 0:56, :] = terms[rows, 0:896]
+        g_send[j, 56:112, :] = terms[rows, 896:1792]
+
     o_y[2]()
     for j in range(NY):
         rows = slice(128 * (j // 2) + 56 * (j % 2), 128 * (j // 2) + 56 * (j % 2) + 56)
@@ -392,26 +417,13 @@
         lo(4, lo_send.at[right, low], lo_recv.at[0, low], 1),
         lo(5, lo_send.at[left, high], lo_recv.at[1, high], 3),
     ]
-    attend(over)
     project(2)
     for c in lo_far:
         c.start()
-    attend(right)
     project(1)
     lo_own[0].start()
-    attend(left)
     project(3)
     lo_own[1].start()
-    attend(x)
-
-    c_x[2]()
-    terms = dot(
-        att[...].reshape(NX * ROWS, 256), cotb[...].reshape(NX * ROWS, width), (((0,), (0,)), ((), ()))
-    ).astype(BF16)
-    for j in range(NY):
-        rows = slice(128 * (j // 2) + 56 * (j % 2), 128 * (j // 2) + 56 * (j % 2) + 56)
-        g_send[j, 0:56, :] = terms[rows, 0:896]
-        g_send[j, 56:112, :] = terms[rows, 896:1792]
 
     def g(k):
         return remote(g_send.at[at_y(k)], g_recv.at[NY - k], gy_s.at[k], gy_r.at[NY - k], dev_y(at_y(k)))
@@ -569,9 +581,9 @@
             pltpu.VMEM((NY, 112, 896), BF16),
             pltpu.VMEM((112, 896), BF16),
             sem((NX,)), sem((NX,)),
-            sem((NX, NY)), sem((NX, NY)), sem((NX,)),
+            sem((NX, 6)), sem((NX, NY)),
             sem((6,)), sem((6,)), sem((6,)), sem((6,)),
-            sem((NY,)), sem((NY,)), sem,
+            sem((6,)), sem((NY,)),
             sem((6,)), sem((6,)), sem((NY,)), sem((NY,)), sem, sem, sem((7,)),
             sem((pieces,)), sem((pieces,)), sem((pieces,)), sem((pieces,)), sem, sem,
             pltpu.SemaphoreType.REGULAR, pltpu.SemaphoreType.REGULAR,

time: 93.3 us -> 92.1 us (0.987)
  the two profiles are of different devices: /device:TPU:130 before, /device:TPU:448 now
where the time goes in v5:
time: 92.1 us; the launch traced here: 91.9 us
  Pallas kernels  90.6 us (98%)
  between operations  1.29 us (1%)
    pallas_call x1, Pallas kernels, on_device(): pl.pallas_call(kernel, out_shape=shapes, in_specs=[hbm] * 7 + [vmem, pl.B...  88.2 us
    pallas_call x1, Pallas kernels, on_device(): pl.pallas_call(hand_out, out_shape=shapes, in_specs=[hbm] * 4, out_specs=...  2.36 us

profile of v5, /device:TPU:448, one launch (start us, length us, event | category | flops | bytes accessed | tf_op | source)
XLA Modules:
  0.0 91.9 jit_solution(1088752609107224621)
XLA Ops:
  1.3 88.2 %shard_map.120 = (bf16[256,1792]{1,0:T(8,128)(2,1)}, f32[56,1792]{1,0:T(8,128)}, f32[256,128]{1,0:T(8,128)}, f32[256,128]{1,0:T(8,128)}) custom-call(bf16[256,1792]{1,0:T(8,128)(2,1)} %bitcast.17, bf16[112,2688]{1,0:T(8,128)(2,1)} %bitcast.20, bf16[56,1792]{1,0:T(8,128)(2,1)} %bitcast.25, bf16[256,1792]{1,0:T(8,128)(2,1)} %bitcast.18, ...), custom_call_target="tpu_custom_call" | custom-call | flops 99999997952 | bytes 5000000 | tf_op jit(solution)/shard_map/pallas_call | solution.py:548
  89.5 2.4 %shard_map.121 = (bf16[256,1792]{1,0:T(8,128)(2,1)}, f32[56,1792]{1,0:T(8,128)}, f32[256,128]{1,0:T(8,128)}, f32[256,128]{1,0:T(8,128)}) custom-call(bf16[256,1792]{1,0:T(8,128)(2,1)} %get-tuple-element.12.out_in, f32[56,1792]{1,0:T(8,128)} %get-tuple-element.13.grad_in, f32[256,128]{1,0:T(8,128)} %get-tuple-element.14.newm_in, ...), custom_call_target="tpu_custom_call" | custom-call | tf_op jit(solution)/shard_map/pallas_call | solution.py:599

commit v6 on v5

--- a/solution.py
+++ b/solution.py
@@ -228,9 +228,10 @@
     ]
     o_y = along_y(lambda yy: oraw.at[yy], lambda j: oy_s.at[j], lambda yy: oy_r.at[yy])
 
-    for k in (2, 1, 3):
+    for k in (1, 3):
         w_x(k).start()
     w_y[0][0]()
+    w_x(2).start()
     from_above(1)
 
     mask = mask_ref[...]
@@ -382,15 +383,6 @@
     o_y[1](2)
     for k in (2, 3):
         attend(at_x(k))
-    c_x[2]()
-    terms = dot(
-        att[...].reshape(NX * ROWS, 256), cotb[...].reshape(NX * ROWS, width), (((0,), (0,)), ((), ()))
-    ).astype(BF16)
-    for j in range(NY):
-        rows = slice(128 * (j // 2) + 56 * (j % 2), 128 * (j // 2) + 56 * (j % 2) + 56)
-        g_send[j, 0:56, :] = terms[rows, 0:896]
-        g_send[j, 56:112, :] = terms[rows, 896:1792]
-
     o_y[2]()
     for j in range(NY):
         rows = slice(128 * (j // 2) + 56 * (j % 2), 128 * (j // 2) + 56 * (j % 2) + 56)
@@ -424,6 +416,16 @@
     lo_own[0].start()
     project(3)
     lo_own[1].start()
+
+    c_x[2]()
+    terms = dot(
+        att[...].reshape(NX * ROWS, 256), cotb[...].reshape(NX * ROWS, width), (((0,), (0,)), ((), ()))
+    ).astype(BF16)
+    for j in range(NY):
+        rows = slice(128 * (j // 2) + 56 * (j % 2), 128 * (j // 2) + 56 * (j % 2) + 56)
+        g_send[j, 0:56, :] = terms[rows, 0:896]
+        g_send[j, 56:112, :] = terms[rows, 896:1792]
+
 
     def g(k):
         return remote(g_send.at[at_y(k)], g_recv.at[NY - k], gy_s.at[k], gy_r.at[NY - k], dev_y(at_y(k)))

time: 92.1 us -> 89.5 us (0.972)
  the two profiles are of different devices: /device:TPU:448 before, /device:TPU:56 now
where the time goes in v6:
time: 89.5 us; the launch traced here: 87.9 us
  Pallas kernels  86.7 us (97%)
  between operations  1.29 us (1%)
    pallas_call x1, Pallas kernels, on_device(): pl.pallas_call(kernel, out_shape=shapes, in_specs=[hbm] * 7 + [vmem, pl.B...  84.3 us
    pallas_call x1, Pallas kernels, on_device(): pl.pallas_call(hand_out, out_shape=shapes, in_specs=[hbm] * 4, out_specs=...  2.36 us

profile of v6, /device:TPU:56, one launch (start us, length us, event | category | flops | bytes accessed | tf_op | source)
XLA Modules:
  0.0 87.9 jit_solution(7450228379912918215)
XLA Ops:
  1.3 84.3 %shard_map.120 = (bf16[256,1792]{1,0:T(8,128)(2,1)}, f32[56,1792]{1,0:T(8,128)}, f32[256,128]{1,0:T(8,128)}, f32[256,128]{1,0:T(8,128)}) custom-call(bf16[256,1792]{1,0:T(8,128)(2,1)} %bitcast.17, bf16[112,2688]{1,0:T(8,128)(2,1)} %bitcast.20, bf16[56,1792]{1,0:T(8,128)(2,1)} %bitcast.25, bf16[256,1792]{1,0:T(8,128)(2,1)} %bitcast.18, ...), custom_call_target="tpu_custom_call" | custom-call | flops 99999997952 | bytes 5000000 | tf_op jit(solution)/shard_map/pallas_call | solution.py:550
  85.6 2.4 %shard_map.121 = (bf16[256,1792]{1,0:T(8,128)(2,1)}, f32[56,1792]{1,0:T(8,128)}, f32[256,128]{1,0:T(8,128)}, f32[256,128]{1,0:T(8,128)}) custom-call(bf16[256,1792]{1,0:T(8,128)(2,1)} %get-tuple-element.12.out_in, f32[56,1792]{1,0:T(8,128)} %get-tuple-element.13.grad_in, f32[256,128]{1,0:T(8,128)} %get-tuple-element.14.newm_in, ...), custom_call_target="tpu_custom_call" | custom-call | tf_op jit(solution)/shard_map/pallas_call | solution.py:601
